TPU v7x, 256 devices: a whole 4x4x8 slice. The times are simulated.
256 devices in a mesh: morton: 32 (over x, y, core), coef: 8 (over z).
Axes of the slice: x: 4, y: 4, z: 8, core: 2. Of those that a mesh axis runs over, the one named last changes fastest.
Arguments:
- multipoles: bfloat16 [262144, 256], P(('morton', 'coef')), may hold values from -6 to 6
- send_rows: int32 [256, 32, 64], P(('morton', 'coef')), may hold values from 0 to 1023
- send_count: int32 [256, 32], P(('morton', 'coef')), may hold values from 0 to 64, as said below
- lists: int32 [262144, 32], P(('morton', 'coef')), may hold values from -1 to 4095, as said below
- operators: bfloat16 [32, 256, 256], replicated, may hold values from -0.0625 to 0.0625
- top_local: float32 [128, 256], P('morton'), may hold values from -6 to 6
- ancestor: int32 [262144], P(('morton', 'coef')), may hold values from 0 to 127
- down_ops: bfloat16 [8, 256, 256], replicated, may hold values from -0.375 to 0.375
Outputs:
- local_exp: float32 [262144, 256], P(('morton', 'coef'))
Inputs may be any that keep to these rules, and one draw needn't show every extreme that they name: send_count of a sub-block to its own range is 0; to ranges within 2 of its own it is at most 64, and exactly 64 to the ranges one above and one below; to farther ranges at most 32, reached for the range 2 + 1 above. An entry of lists points into received only at slots below the matching send_count.
All inputs are finite; a program needn't handle non-finite values.
Results may differ from a plain program's by a relative error of at most 0.0022.
Values may be sent and summed in bfloat16 or wider, within the bound.
No kernel may reach another device: no remote copies, remote signals or barrier semaphores. Data moves between devices by JAX's collectives and lax.ppermute only.
A program may use at most 64 MiB of HBM per device.

v0:
```python
import jax
import jax.numpy as jnp
from jax import lax
from jax.sharding import PartitionSpec as P


def with_halo(block, sides, width):
    for axis, dim in sides:
        count = lax.axis_size(axis)
        forward = [(i, i + 1) for i in range(count - 1)]
        backward = [(target, source) for source, target in forward]
        low = lax.ppermute(
            lax.slice_in_dim(block, block.shape[dim] - width, None, axis=dim), axis, forward
        )
        high = lax.ppermute(lax.slice_in_dim(block, 0, width, axis=dim), axis, backward)
        block = jnp.concatenate([low, block, high], axis=dim)
    return block


def on_device(multipoles, send_rows, send_count, lists, operators, top_local, ancestor, down_ops):
    leaf_rows = multipoles.shape[0]
    coefs = multipoles.shape[1]
    slots = operators.shape[0]
    capacity = send_rows.shape[2]
    peers = lax.axis_size("morton")
    nearby = with_halo(multipoles, (("coef", 0),), leaf_rows // 2)
    picks = send_rows[0]
    live = lax.broadcasted_iota(jnp.int32, picks.shape, 1) < send_count[0][:, None]
    outgoing = jnp.where(live[:, :, None], multipoles[picks], jnp.zeros((), multipoles.dtype))
    incoming = lax.all_to_all(outgoing, "morton", split_axis=0, concat_axis=0, tiled=True)
    zero_row = jnp.zeros((1, coefs), multipoles.dtype)
    table = jnp.concatenate([nearby, incoming.reshape(peers * capacity, coefs), zero_row], 0)
    blank = table.shape[0] - 1
    entries = jnp.where(lists >= 0, lists, blank).T
    group = 8
    far = jnp.zeros((leaf_rows, coefs), jnp.float32)
    for first in range(0, slots, group):
        block_sources = table[entries[first : first + group]]
        far = far + lax.dot_general(
            block_sources,
            operators[first : first + group],
            (((0, 2), (0, 1)), ((), ())),
            preferred_element_type=jnp.float32,
        )
    whole_top = lax.all_gather(top_local, "morton", axis=0, tiled=True)
    top_ids = lax.broadcasted_iota(jnp.int32, (1, whole_top.shape[0]), 1)
    onehot = (ancestor[:, None] == top_ids).astype(jnp.float32)
    lifted = jnp.dot(
        onehot, whole_top, precision=lax.Precision.HIGHEST, preferred_element_type=jnp.float32
    ).astype(jnp.bfloat16)
    inherited = jnp.einsum(
        "nop,opq->noq",
        lifted.reshape(leaf_rows // 8, 8, coefs),
        down_ops,
        preferred_element_type=jnp.float32,
    )
    return far + inherited.reshape(leaf_rows, coefs)


def solution(mesh):
    placed = (
        P(("morton", "coef"), None),
        P(("morton", "coef"), None, None),
        P(("morton", "coef"), None),
        P(("morton", "coef"), None),
        P(),
        P("morton", None),
        P(("morton", "coef")),
        P(),
    )
    return jax.shard_map(
        on_device,
        mesh=mesh,
        in_specs=placed,
        out_specs=P(("morton", "coef"), None),
        check_vma=False,
    )
```

profile of v0, /device:TPU:1, one launch (start us, length us, event | category | flops | bytes accessed | tf_op | source)
XLA Modules:
  0.0 207.8 jit_solution(7856937545572054513)
XLA Ops:
  0.0 0.0 copy-start
  0.0 0.0 copy-start.1
  0.0 1.9 fusion.16
  1.9 5.1 %collective-permute-start = (bf16[512,256]{1,0:T(8,128)(2,1)S(1)}, bf16[512,256]{1,0:T(8,128)(2,1)}, u32[]{:S(2)}, u32[]{:S(2)}) collective-permute-start(bf16[512,256]{1,0:T(8,128)(2,1)S(1)} %get-tuple-element.6), channel_id=1, source_target_pairs={{0,1},{1,2},{2,3},{3,4},{4,5},{5,6},{6,7},{8,9},{9,10},{10,11},{11... | collective-permute-start | bytes 786440 | tf_op jit(solution)/shard_map/ppermute | solution.py:12
  7.0 1.3 collective-permute-start.1
  8.2 0.7 compare_select_fusion.5
  9.0 0.1 reshape.65
  9.1 0.0 copy-done.1
  9.1 0.0 copy-start.9
  9.1 7.5 %gather_fusion = bf16[2048,256]{1,0:T(8,128)(2,1)S(1)} fusion(bf16[1024,256]{1,0:T(8,128)(2,1)S(1)} %copy-done.1, s32[2048]{0:T(1024)S(1)} %broadcast_clamp_fusion), kind=kCustom, calls=%fused_computation | custom fusion | bytes 2105344 | tf_op jit(solution)/shard_map/gather | solution.py:29
  16.6 0.0 copy-start.6
  16.6 0.0 copy-start.8
  16.6 0.0 copy-start.7
  16.6 0.0 copy-done.9
  16.6 0.1 iota_compare_fusion.2
  16.7 1.2 broadcast_select_fusion
  17.9 8.1 %all-to-all-start = ((bf16[32,64,256]{2,1,0:T(8,128)(2,1)}), bf16[32,64,256]{2,1,0:T(8,128)(2,1)}, u32[]{:S(2)}, u32[]{:S(2)}) async-start(bf16[32,64,256]{2,1,0:T(8,128)(2,1)} %broadcast_select_fusion), calls=%async_computation | async-start | bytes 2097152 | tf_op jit(solution)/shard_map/all_to_all | solution.py:30
  26.0 0.0 copy-done.6
  26.0 0.0 copy-done.8
  26.0 32.3 %all-gather = f32[32,4,256]{2,1,0:T(4,128)S(1)} all-gather(f32[1,4,256]{2,1,0:T(4,128)S(1)} %bitcast.63), channel_id=1, replica_groups=mesh['morton'=32,'coef'=8] {'morton'}, dimensions={0}, use_global_device_ids=true | all-gather | bytes 135168 | tf_op jit(solution)/shard_map/all_gather | solution.py:45
  58.4 0.0 copy-done.7
  58.4 0.6 fusion.4
  59.0 0.0 copy-done
  59.0 1.3 convolution_bitcast_fusion.4
  60.4 0.0 collective-permute-done
  60.4 1.0 constant_dynamic-update-slice_fusion.4
  61.4 1.1 constant_dynamic-update-slice_fusion.3
  62.5 0.0 collective-permute-done.1
  62.5 0.0 all-to-all-done
  62.5 1.3 constant_dynamic-update-slice_fusion.1
  63.8 33.1 %gather_fusion.2 = bf16[8192,256]{1,0:T(8,128)(2,1)} fusion(bf16[4097,256]{1,0:T(8,128)(2,1)S(1)} %constant_dynamic-update-slice_fusion, s32[8192]{0:T(1024)S(1)} %get-tuple-element.13), kind=kCustom, calls=%fused_computation.2 | custom fusion | bytes 8421376 | tf_op jit(solution)/shard_map/gather | solution.py:38
  96.9 33.1 %gather_fusion.1 = bf16[8192,256]{1,0:T(8,128)(2,1)} fusion(bf16[4097,256]{1,0:T(8,128)(2,1)S(1)} %constant_dynamic-update-slice_fusion, s32[8192]{0:T(1024)S(1)} %get-tuple-element.14), kind=kCustom, calls=%fused_computation.1 | custom fusion | bytes 8421376 | tf_op jit(solution)/shard_map/gather | solution.py:38
  130.0 33.1 %gather_fusion.3 = bf16[8192,256]{1,0:T(8,128)(2,1)} fusion(bf16[4097,256]{1,0:T(8,128)(2,1)S(1)} %constant_dynamic-update-slice_fusion, s32[8192]{0:T(1024)S(1)} %get-tuple-element.12), kind=kCustom, calls=%fused_computation.3 | custom fusion | bytes 8421376 | tf_op jit(solution)/shard_map/gather | solution.py:38
  163.1 33.1 %gather_fusion.4 = bf16[8192,256]{1,0:T(8,128)(2,1)} fusion(bf16[4097,256]{1,0:T(8,128)(2,1)S(1)} %constant_dynamic-update-slice_fusion, s32[8192]{0:T(1024)S(1)} %get-tuple-element.11), kind=kCustom, calls=%fused_computation.4 | custom fusion | bytes 8421376 | tf_op jit(solution)/shard_map/gather | solution.py:38
  196.2 0.0 copy-start.4
  196.2 0.0 copy-start.10
  196.2 3.9 %convolution_bitcast_fusion.2 = f32[1024,256]{1,0:T(8,128)S(1)} fusion(bf16[8,1024,256]{2,1,0:T(8,128)(2,1)} %bitcast.60, bf16[32,256,256]{2,1,0:T(8,128)(2,1)} %param.12), kind=kOutput, calls=%fused_computation.7 | convolution fusion | flops 1073741824 | bytes 6291456 | tf_op jit(solution)/shard_map/dot_general | solution.py:39
  200.1 0.0 copy-start.3
  200.1 0.0 copy-done.4
  200.1 2.6 %fusion = f32[1024,256]{1,0:T(8,128)S(1)} fusion(f32[1024,256]{1,0:T(8,128)S(1)} %convolution_bitcast_fusion.2, bf16[8,1024,256]{2,1,0:T(8,128)(2,1)S(1)} %bitcast.62, bf16[32,256,256]{2,1,0:T(8,128)(2,1)} %param.12), kind=kOutput, calls=%fused_computation.10 | convolution fusion | flops 1074003968 | bytes 7340032 | tf_op jit(solution)/shard_map/dot_general | solution.py:39
  202.8 0.0 copy-start.2
  202.8 0.0 copy-start.5
  202.8 0.0 copy-done.10
  202.8 0.2 copy-done.3
  203.0 1.2 fusion.1
  204.2 0.8 copy-done.2
  205.0 0.2 copy-done.5
  205.2 2.6 %fusion.3 = f32[1024,256]{1,0:T(8,128)} fusion(f32[1024,256]{1,0:T(8,128)S(1)} %fusion.1, bf16[8,1024,256]{2,1,0:T(8,128)(2,1)S(1)} %bitcast.59, f32[128,8,256]{2,0,1:T(8,128)S(1)} %copy-done.5, bf16[32,256,256]{2,1,0:T(8,128)(2,1)S(1)} %copy-done.10), kind=kOutput, calls=%fused_computation.13 | convolution fusion | flops 1074266112 | bytes 8388608 | tf_op jit(solution)/shard_map/dot_general | solution.py:39
  (8 shorter events, 0.2 us)
Async XLA Ops:
  0.0 59.0 %copy-start = (bf16[8,256,256]{2,1,0:T(8,128)(2,1)S(1)}, bf16[8,256,256]{2,1,0:T(8,128)(2,1)}, u32[]{:S(2)}) copy-start(bf16[8,256,256]{2,1,0:T(8,128)(2,1)} %param.15) | copy-start | bytes 3145732
  0.0 9.1 %copy-start.1 = (bf16[1024,256]{1,0:T(8,128)(2,1)S(1)}, bf16[1024,256]{1,0:T(8,128)(2,1)}, u32[]{:S(2)}) copy-start(bf16[1024,256]{1,0:T(8,128)(2,1)} %param.8) | copy-start | bytes 1572868
  1.9 58.5 %collective-permute-start = (bf16[512,256]{1,0:T(8,128)(2,1)S(1)}, bf16[512,256]{1,0:T(8,128)(2,1)}, u32[]{:S(2)}, u32[]{:S(2)}) collective-permute-start(bf16[512,256]{1,0:T(8,128)(2,1)S(1)} %get-tuple-element.6), channel_id=1, source_target_pairs={{0,1},{1,2},{2,3},{3,4},{4,5},{5,6},{6,7},{8,9},{9,10},{10,11},{11... | collective-permute-start | bytes 786440 | tf_op jit(solution)/shard_map/ppermute | solution.py:12
  7.0 55.5 %collective-permute-start.1 = (bf16[512,256]{1,0:T(8,128)(2,1)}, bf16[512,256]{1,0:T(8,128)(2,1)S(1)}, u32[]{:S(2)}, u32[]{:S(2)}) collective-permute-start(bf16[512,256]{1,0:T(8,128)(2,1)} %get-tuple-element.5), channel_id=1, source_target_pairs={{1,0},{2,1},{3,2},{4,3},{5,4},{6,5},{7,6},{9,8},{10,9},{11,10},{12... | collective-permute-start | bytes 786440 | tf_op jit(solution)/shard_map/ppermute | solution.py:15
  9.1 7.5 %copy-start.9 = (s32[1,32]{1,0:T(1,128)S(1)}, s32[1,32]{1,0:T(1,128)}, u32[]{:S(2)}) copy-start(s32[1,32]{1,0:T(1,128)} %param.10) | copy-start | bytes 388
  16.6 9.4 %copy-start.6 = (s32[1024,32]{0,1:T(8,128)S(1)}, s32[1024,32]{0,1:T(8,128)}, u32[]{:S(2)}) copy-start(s32[1024,32]{0,1:T(8,128)} %param.11) | copy-start | bytes 393220
  16.6 9.5 %copy-start.8 = (f32[4,256]{1,0:T(4,128)S(1)}, f32[4,256]{1,0:T(4,128)}, u32[]{:S(2)}) copy-start(f32[4,256]{1,0:T(4,128)} %param.13) | copy-start | bytes 12292
  16.6 41.8 %copy-start.7 = (s32[1024]{0:T(1024)S(1)}, s32[1024]{0:T(1024)}, u32[]{:S(2)}) copy-start(s32[1024]{0:T(1024)} %param.14) | copy-start | bytes 12292
  17.9 44.6 %all-to-all-start = ((bf16[32,64,256]{2,1,0:T(8,128)(2,1)}), bf16[32,64,256]{2,1,0:T(8,128)(2,1)}, u32[]{:S(2)}, u32[]{:S(2)}) async-start(bf16[32,64,256]{2,1,0:T(8,128)(2,1)} %broadcast_select_fusion), calls=%async_computation | async-start | bytes 2097152 | tf_op jit(solution)/shard_map/all_to_all | solution.py:30
  196.2 3.9 %copy-start.4 = (bf16[8192,256]{1,0:T(8,128)(2,1)S(1)}, bf16[8192,256]{1,0:T(8,128)(2,1)}, u32[]{:S(2)}) copy-start(bf16[8192,256]{1,0:T(8,128)(2,1)} %gather_fusion.1) | copy-start | bytes 12582916
  196.2 6.6 %copy-start.10 = (bf16[32,256,256]{2,1,0:T(8,128)(2,1)S(1)}, bf16[32,256,256]{2,1,0:T(8,128)(2,1)}, u32[]{:S(2)}) copy-start(bf16[32,256,256]{2,1,0:T(8,128)(2,1)} %param.12) | copy-start | bytes 12582916
  200.1 2.9 %copy-start.3 = (bf16[8192,256]{1,0:T(8,128)(2,1)S(1)}, bf16[8192,256]{1,0:T(8,128)(2,1)}, u32[]{:S(2)}) copy-start(bf16[8192,256]{1,0:T(8,128)(2,1)} %gather_fusion.3) | copy-start | bytes 12582916
  202.8 2.2 %copy-start.2 = (bf16[8192,256]{1,0:T(8,128)(2,1)S(1)}, bf16[8192,256]{1,0:T(8,128)(2,1)}, u32[]{:S(2)}) copy-start(bf16[8192,256]{1,0:T(8,128)(2,1)} %gather_fusion.4) | copy-start | bytes 12582916
  202.8 2.5 %copy-start.5 = (f32[128,8,256]{2,0,1:T(8,128)S(1)}, f32[128,8,256]{2,0,1:T(8,128)}, u32[]{:S(2)}) copy-start(f32[128,8,256]{2,0,1:T(8,128)} %convolution_bitcast_fusion.4) | copy-start | bytes 3145732
where the time goes:
time: 209 us; the launch traced here: 208 us
  local copies, waits for them, and re-layouts  146 us (70%)
  blocking collectives  32.3 us (15%)
  starting transfers between devices  14.4 us (7%)
  matrix products  12.2 us (6%)
  other arithmetic  2.09 us (1%)
    gather x4, local copies, waits for them, and re-layouts, on_device(): block_sources = table[entries[first:first + group]]  132 us
    all_gather x1, blocking collectives, on_device(): whole_top = lax.all_gather(top_local, 'morton', axis=0, tiled=True)  32.3 us
    dot_general x4, matrix products, on_device(): lax.dot_general(block_sources, operators[first:first + group], (((0, 2),...  10.3 us
    all_to_all x1, starting transfers between devices, on_device(): lax.all_to_all(outgoing, 'morton', split_axis=0, concat_axis=0, tiled=True)  8.09 us
    gather x1, local copies, waits for them, and re-layouts, on_device(): multipoles[picks]  7.5 us
    ppermute x1, starting transfers between devices, with_halo(): lax.ppermute(lax.slice_in_dim(block, block.shape[dim] - width, None, axis...  5.07 us
    unnamed x27, local copies, waits for them, and re-layouts  4.63 us
  transfers between devices with their start and end apart: 3, of which 0 were waited for; matrix products, arithmetic and copies ran while one was open for 7% of the time, Pallas kernels for 0%

commit v1 on v0

v1 whole, which is shorter than its diff:
```python
import functools

import jax
import jax.numpy as jnp
from jax import lax
from jax.experimental import pallas as pl
from jax.experimental.pallas import tpu as pltpu
from jax.sharding import PartitionSpec as P

NEAR = (-2, -1, 1, 2)
SEND = 64
FAR_SLOTS = 32
LANES = 128
TARGETS = 256
CLASSES = 8
ROW_BLOCK = 32
WINDOW = 4096
BLANK = 2 * WINDOW
TOP_BASE = BLANK + 16


def send_kernel(peers, me_ref, pick_ref, cells_ref, top_ref, split_ref, out_ref, near_ref, table, rows):
    count = cells_ref.shape[0]
    step = 256
    for first in range(0, count, step):
        wide = cells_ref[first : first + step, :].astype(jnp.float32)
        table[pl.ds(2 * first, step, stride=2), :] = wide[:, :LANES]
        table[pl.ds(2 * first + 1, step, stride=2), :] = wide[:, LANES:]
    pitch = 2 * FAR_SLOTS + top_ref.shape[0]
    for peer in range(peers):
        for slot in range(FAR_SLOTS):
            source = pl.multiple_of(pick_ref[peer * SEND + slot], 2)
            rows[pl.ds(peer * pitch + 2 * slot, 2), :] = table[pl.ds(source, 2), :]
        rows[pl.ds(peer * pitch + 2 * FAR_SLOTS, top_ref.shape[0]), :] = top_ref[...]
        out_ref[peer] = rows[peer * pitch : (peer + 1) * pitch, :].astype(jnp.bfloat16)
    base = peers * pitch
    for near, distance in enumerate(NEAR):
        first = jnp.clip(me_ref[0] + distance, 0, peers - 1) * SEND + FAR_SLOTS
        for slot in range(FAR_SLOTS):
            source = pl.multiple_of(pick_ref[first + slot], 2)
            rows[pl.ds(base + 2 * slot, 2), :] = table[pl.ds(source, 2), :]
        near_ref[near] = rows[base : base + 2 * FAR_SLOTS, :].astype(jnp.bfloat16)
        base += 2 * FAR_SLOTS
    for first in range(0, 2 * count, 512):
        split_ref[first : first + 512, :] = table[first : first + 512, :].astype(jnp.bfloat16)


def main_kernel(
    peers,
    me_ref,
    index_ref,
    low_ref,
    own_ref,
    high_ref,
    incoming_ref,
    near_ref,
    ops_ref,
    down_ref,
    out_ref,
    table,
    index_a,
    index_b,
    index_top,
    picked_a,
    picked_b,
    total,
    index_sem,
):
    chunk = TARGETS * CLASSES
    slots = ops_ref.shape[0]
    groups = slots // CLASSES
    leaves = out_ref.shape[0]
    steps = leaves * slots // chunk
    indices = (index_a, index_b)
    picked = (picked_a, picked_b)

    def fetch(step, slot):
        first = pl.multiple_of(step * chunk, chunk)
        return pltpu.make_async_copy(
            index_ref.at[pl.ds(first, chunk)], indices[slot], index_sem.at[slot]
        )

    top_fetch = pltpu.make_async_copy(
        index_ref.at[pl.ds(leaves * slots, leaves)], index_top, index_sem.at[2]
    )
    top_fetch.start()
    fetch(0, 0).start()
    fetch(1, 1).start()

    def widen(source, rows, target):
        part = 512
        for first in range(0, rows, part):
            table[target + first : target + first + part, :] = source[
                first : first + part, :
            ].astype(jnp.float32)

    rim = low_ref.shape[0]
    own = own_ref.shape[0]
    widen(low_ref, rim, 0)
    widen(own_ref, own, rim)
    widen(high_ref, rim, rim + own)
    remote = 2 * rim + own
    per_peer = (BLANK - remote) // peers
    slab = 2 * FAR_SLOTS
    tops = incoming_ref.shape[1] - slab
    for peer in range(peers):
        part = incoming_ref[peer].astype(jnp.float32)
        table[remote + peer * per_peer : remote + peer * per_peer + slab, :] = part[:slab]
        table[TOP_BASE + peer * tops : TOP_BASE + (peer + 1) * tops, :] = part[slab:]
    table[BLANK:TOP_BASE, :] = jnp.zeros((TOP_BASE - BLANK, LANES), jnp.float32)
    for near, distance in enumerate(NEAR):
        peer = me_ref[0] - distance

        @pl.when((peer >= 0) & (peer < peers))
        def _():
            first = pl.multiple_of(remote + peer * per_peer + slab, slab)
            table[pl.ds(first, slab), :] = near_ref[near].astype(jnp.float32)

    def gather(where, position, target):
        source = pl.multiple_of(where[position], 2)
        target[pl.ds(2 * position, 2), :] = table[pl.ds(source, 2), :]

    def halves(rows, first, count):
        return [
            rows[pl.ds(2 * first + half, count, stride=2), :].astype(jnp.bfloat16)
            for half in range(2)
        ]

    top_fetch.wait()
    octants = down_ref.shape[0]
    share = leaves // octants
    for position in range(leaves):
        gather(index_top, position, picked_a)
    for octant in range(octants):
        lhs = jnp.concatenate(halves(picked_a, octant * share, share), axis=1)
        inherited = jnp.dot(lhs, down_ref[octant], preferred_element_type=jnp.float32)
        for half in range(2):
            total.at[half][pl.ds(octant, share, stride=octants), :] = inherited[
                :, half * LANES : (half + 1) * LANES
            ]

    def part_step(step, slot):
        fetch(step, slot).wait()
        for first in range(0, TARGETS, ROW_BLOCK):
            for member in range(CLASSES):
                for row in range(first, first + ROW_BLOCK):
                    gather(indices[slot], member * TARGETS + row, picked[slot])
        lhs = jnp.concatenate(
            [x for member in range(CLASSES) for x in halves(picked[slot], member * TARGETS, TARGETS)],
            axis=1,
        )
        group = step % groups
        rhs = ops_ref[pl.ds(group * CLASSES, CLASSES)].reshape(CLASSES * 2 * LANES, 2 * LANES)
        product = jnp.dot(lhs, rhs, preferred_element_type=jnp.float32)
        rows = pl.ds(pl.multiple_of(step // groups * TARGETS, TARGETS), TARGETS)
        for half in range(2):
            total[half, rows, :] += product[:, half * LANES : (half + 1) * LANES]

        @pl.when(step + 2 < steps)
        def _():
            fetch(step + 2, slot).start()

    def pair(index, carry):
        part_step(2 * index, 0)
        part_step(2 * index + 1, 1)
        return carry

    lax.fori_loop(0, steps // 2, pair, 0)
    for half in range(2):
        out_ref[:, half * LANES : (half + 1) * LANES] = total[half]


def on_device(multipoles, send_rows, send_count, lists, operators, top_local, ancestor, down_ops):
    leaves, coefs = multipoles.shape
    slots = operators.shape[0]
    peers = lax.axis_size("morton")
    me = lax.axis_index("morton")
    pick_rows = (2 * send_rows).reshape(-1)
    top_rows = top_local.reshape(-1, LANES)
    pitch = 2 * FAR_SLOTS + top_rows.shape[0]
    total_rows = peers * pitch + len(NEAR) * 2 * FAR_SLOTS
    vmem = pl.BlockSpec(memory_space=pltpu.VMEM)
    smem = pl.BlockSpec(memory_space=pltpu.SMEM)
    own, outgoing, near = pl.pallas_call(
        functools.partial(send_kernel, peers),
        out_shape=(
            jax.ShapeDtypeStruct((2 * leaves, LANES), jnp.bfloat16),
            jax.ShapeDtypeStruct((peers, pitch, LANES), jnp.bfloat16),
            jax.ShapeDtypeStruct((len(NEAR), 2 * FAR_SLOTS, LANES), jnp.bfloat16),
        ),
        in_specs=[smem, smem, vmem, vmem],
        out_specs=(vmem, vmem, vmem),
        scratch_shapes=[
            pltpu.VMEM((2 * leaves, LANES), jnp.float32),
            pltpu.VMEM((total_rows, LANES), jnp.float32),
        ],
        compiler_params=pltpu.CompilerParams(vmem_limit_bytes=16 * 2**20),
        name="send_rows",
    )(me[None], pick_rows, multipoles, top_rows)
    incoming = lax.all_to_all(outgoing, "morton", split_axis=0, concat_axis=0, tiled=True)
    ranks = lax.axis_size("coef")
    forward = [(i, i + 1) for i in range(ranks - 1)]
    backward = [(i + 1, i) for i in range(ranks - 1)]
    low = lax.ppermute(own[leaves:], "coef", forward)
    high = lax.ppermute(own[:leaves], "coef", backward)
    extras = [
        lax.ppermute(
            near[i],
            "morton",
            [(source, source + d) for source in range(peers) if 0 <= source + d < peers],
        )
        for i, d in enumerate(NEAR)
    ]
    near_in = jnp.stack(extras)
    entries = jnp.where(lists >= 0, 2 * lists, BLANK).T
    entries = entries.reshape(slots // CLASSES, CLASSES, leaves // TARGETS, TARGETS)
    entries = entries.transpose(2, 0, 1, 3).reshape(-1)
    octants = down_ops.shape[0]
    parents = (TOP_BASE + 2 * ancestor).reshape(leaves // octants, octants).T.reshape(-1)
    index = jnp.concatenate([entries, parents])
    chunk = TARGETS * CLASSES
    return pl.pallas_call(
        functools.partial(main_kernel, peers),
        out_shape=jax.ShapeDtypeStruct((leaves, coefs), jnp.float32),
        in_specs=[smem] + [vmem] * 8,
        out_specs=vmem,
        scratch_shapes=[
            pltpu.VMEM((TOP_BASE + peers * top_rows.shape[0], LANES), jnp.float32),
            pltpu.SMEM((chunk,), jnp.int32),
            pltpu.SMEM((chunk,), jnp.int32),
            pltpu.SMEM((leaves,), jnp.int32),
            pltpu.VMEM((2 * chunk, LANES), jnp.float32),
            pltpu.VMEM((2 * chunk, LANES), jnp.float32),
            pltpu.VMEM((2, leaves, LANES), jnp.float32),
            pltpu.SemaphoreType.DMA((3,)),
        ],
        compiler_params=pltpu.CompilerParams(vmem_limit_bytes=48 * 2**20),
        name="far_field",
    )(me[None], index, low, own, high, incoming, near_in, operators, down_ops)


def solution(mesh):
    placed = (
        P(("morton", "coef"), None),
        P(("morton", "coef"), None, None),
        P(("morton", "coef"), None),
        P(("morton", "coef"), None),
        P(),
        P("morton", None),
        P(("morton", "coef")),
        P(),
    )
    return jax.shard_map(
        on_device,
        mesh=mesh,
        in_specs=placed,
        out_specs=P(("morton", "coef"), None),
        check_vma=False,
    )
```

time: 209 us -> 72.5 us (0.35)
  the two profiles are of different devices: /device:TPU:1 before, /device:TPU:134 now
where the time goes in v1:
time: 72.5 us; the launch traced here: 72 us
  Pallas kernels  33.8 us (47%)
  starting transfers between devices  27.9 us (38%)
  waiting for transfers between devices  5.59 us (8%)
  other arithmetic  2.36 us (3%)
  local copies, waits for them, and re-layouts  2.17 us (3%)
    pallas_call x1, Pallas kernels, on_device(): pl.pallas_call(functools.partial(main_kernel, peers), out_shape=jax.Shape...  31.3 us
    ppermute x4, starting transfers between devices, on_device(): lax.ppermute(near[i], 'morton', [(source, source + d) for source in range...  14.5 us
    all_to_all x1, starting transfers between devices, on_device(): lax.all_to_all(outgoing, 'morton', split_axis=0, concat_axis=0, tiled=True)  7.6 us
    ppermute x1, waiting for transfers between devices, on_device(): low = lax.ppermute(own[leaves:], 'coef', forward)  5.12 us
    ppermute x1, starting transfers between devices, on_device(): low = lax.ppermute(own[leaves:], 'coef', forward)  3.82 us
    pallas_call x1, Pallas kernels, on_device(): pl.pallas_call(functools.partial(send_kernel, peers), out_shape=(jax.Shap...  2.52 us
    ppermute x1, starting transfers between devices, on_device(): high = lax.ppermute(own[:leaves], 'coef', backward)  2.03 us
  transfers between devices with their start and end apart: 7, of which 2 were waited for; matrix products, arithmetic and copies ran while one was open for 3% of the time, Pallas kernels for 0%

profile of v1, /device:TPU:134, one launch (start us, length us, event | category | flops | bytes accessed | tf_op | source)
XLA Modules:
  0.0 72.0 jit_solution(11013478725263443557)
XLA Ops:
  0.0 0.0 copy-start
  0.0 0.8 %reshape.23.top_ref = f32[8,128]{1,0:T(8,128)S(1)} reshape(f32[4,256]{1,0:T(4,128)} %param.12) | data formatting | bytes 8192 | tf_op jit(solution)/shard_map/reshape | solution.py:179
  0.8 0.7 broadcast_multiply_fusion
  1.5 0.1 reshape.22.pick_ref
  1.6 0.0 copy-start.1
  1.6 1.0 %copy-done.1 = bf16[1024,256]{1,0:T(8,128)(2,1)S(1)} copy-done((bf16[1024,256]{1,0:T(8,128)(2,1)S(1)}, bf16[1024,256]{1,0:T(8,128)(2,1)}, u32[]{:S(2)}) %copy-start.1) | copy-done | bytes 524312
  2.6 2.5 %send_rows.1 = (bf16[2048,128]{1,0:T(8,128)(2,1)S(1)}, bf16[32,72,128]{2,1,0:T(8,128)(2,1)}, bf16[4,64,128]{2,1,0:T(8,128)(2,1)S(1)}) custom-call(s32[1]{0:T(128)} %bitcast.me_ref, s32[2048]{0:T(1024)S(1)} %reshape.22.pick_ref, bf16[1024,256]{1,0:T(8,128)(2,1)S(1)} %copy-done.1, f32[8,128]{1,0:T(8,128)S(1)} %reshape.23.top_ref), custom_call_target="tpu_custom_call" | custom-call | tf_op jit(solution)/shard_map/send_rows/pallas_call | solution.py:184
  5.1 7.6 %all-to-all-start = ((bf16[32,72,128]{2,1,0:T(8,128)(2,1)}), bf16[32,72,128]{2,1,0:T(8,128)(2,1)S(1)}, u32[]{:S(2)}, u32[]{:S(2)}) async-start(bf16[32,72,128]{2,1,0:T(8,128)(2,1)} %get-tuple-element.9), calls=%async_computation | async-start | bytes 1179648 | tf_op jit(solution)/shard_map/all_to_all | solution.py:200
  12.8 4.9 %collective-permute-start.2 = (bf16[64,128]{1,0:T(8,128)(2,1)S(1)}, bf16[64,128]{1,0:T(8,128)(2,1)S(1)}, u32[]{:S(2)}, u32[]{:S(2)}) collective-permute-start(bf16[64,128]{1,0:T(8,128)(2,1)S(1)} %get-tuple-element.13), channel_id=1, source_target_pairs={{16,0},{24,8},{32,16},{40,24},{48,32},{56,40},{64,48},{72,56},{80,... | collective-permute-start | bytes 49160 | tf_op jit(solution)/shard_map/ppermute | solution.py:207
  17.6 1.9 %collective-permute-start.5 = (bf16[64,128]{1,0:T(8,128)(2,1)S(1)}, bf16[64,128]{1,0:T(8,128)(2,1)S(1)}, u32[]{:S(2)}, u32[]{:S(2)}) collective-permute-start(bf16[64,128]{1,0:T(8,128)(2,1)S(1)} %get-tuple-element.14), channel_id=1, source_target_pairs={{0,16},{8,24},{16,32},{24,40},{32,48},{40,56},{48,64},{56,72},{64,... | collective-permute-start | bytes 49160 | tf_op jit(solution)/shard_map/ppermute | solution.py:207
  19.6 1.9 %collective-permute-start.4 = (bf16[64,128]{1,0:T(8,128)(2,1)S(1)}, bf16[64,128]{1,0:T(8,128)(2,1)S(1)}, u32[]{:S(2)}, u32[]{:S(2)}) collective-permute-start(bf16[64,128]{1,0:T(8,128)(2,1)S(1)} %get-tuple-element.15), channel_id=1, source_target_pairs={{0,8},{8,16},{16,24},{24,32},{32,40},{40,48},{48,56},{56,64},{64,7... | collective-permute-start | bytes 49160 | tf_op jit(solution)/shard_map/ppermute | solution.py:207
  21.5 5.8 %collective-permute-start.3 = (bf16[64,128]{1,0:T(8,128)(2,1)S(1)}, bf16[64,128]{1,0:T(8,128)(2,1)S(1)}, u32[]{:S(2)}, u32[]{:S(2)}) collective-permute-start(bf16[64,128]{1,0:T(8,128)(2,1)S(1)} %get-tuple-element.16), channel_id=1, source_target_pairs={{8,0},{16,8},{24,16},{32,24},{40,32},{48,40},{56,48},{64,56},{72,6... | collective-permute-start | bytes 49160 | tf_op jit(solution)/shard_map/ppermute | solution.py:207
  27.3 2.0 %collective-permute-start.1 = (bf16[1024,128]{1,0:T(8,128)(2,1)S(1)}, bf16[1024,128]{1,0:T(8,128)(2,1)S(1)}, u32[]{:S(2)}, u32[]{:S(2)}) collective-permute-start(bf16[1024,128]{1,0:T(8,128)(2,1)S(1)} %get-tuple-element.11), channel_id=1, source_target_pairs={{1,0},{2,1},{3,2},{4,3},{5,4},{6,5},{7,6},{9,8},{10,9},{11,10},{12... | collective-permute-start | bytes 786440 | tf_op jit(solution)/shard_map/ppermute | solution.py:205
  29.3 0.9 %multiply_select_fusion = s32[1024,32]{0,1:T(8,128)S(1)} fusion(s32[1024,32]{0,1:T(8,128)} %param.10), kind=kLoop, calls=%fused_computation.1 | loop fusion | flops 98304 | bytes 262144 | tf_op jit(solution)/shard_map/jit(_where)/select_n | solution.py:215
  30.3 0.7 multiply_add_fusion
  31.0 0.1 reshape.20
  31.1 0.1 copy.10
  31.2 0.0 collective-permute-done.2
  31.2 3.8 %collective-permute-start = (bf16[1024,128]{1,0:T(8,128)(2,1)S(1)}, bf16[1024,128]{1,0:T(8,128)(2,1)S(1)}, u32[]{:S(2)}, u32[]{:S(2)}) collective-permute-start(bf16[1024,128]{1,0:T(8,128)(2,1)S(1)} %get-tuple-element.12), channel_id=1, source_target_pairs={{0,1},{1,2},{2,3},{3,4},{4,5},{5,6},{6,7},{8,9},{9,10},{10,11},{11... | collective-permute-start | bytes 786440 | tf_op jit(solution)/shard_map/ppermute | solution.py:204
  35.1 0.0 collective-permute-done.5
  35.1 0.0 collective-permute-done.4
  35.1 0.0 collective-permute-done.3
  35.1 0.5 collective-permute-done.1.high_ref
  35.6 5.1 %collective-permute-done.low_ref = bf16[1024,128]{1,0:T(8,128)(2,1)S(1)} collective-permute-done((bf16[1024,128]{1,0:T(8,128)(2,1)S(1)}, bf16[1024,128]{1,0:T(8,128)(2,1)S(1)}, u32[]{:S(2)}, u32[]{:S(2)}) %collective-permute-start) | collective-permute-done | bytes 262176 | tf_op jit(solution)/shard_map/ppermute | solution.py:204
  40.7 0.0 all-to-all-done.incoming_ref
  40.7 0.0 copy-done
  40.7 31.3 %far_field.1 = f32[1024,256]{1,0:T(8,128)} custom-call(s32[1]{0:T(128)} %bitcast.me_ref, s32[33792]{0:T(1024)S(1)} %pad_add_fusion.index_ref, bf16[1024,128]{1,0:T(8,128)(2,1)S(1)} %collective-permute-done.low_ref, bf16[2048,128]{1,0:T(8,128)(2,1)S(1)} %get-tuple-element.8.own_ref, bf16[1024,128]{1,0:T(8,128)(2,1)S(1)} %collective-permute-done.1.high_ref, ...), custom_call_target="tpu_custom_call" | custom-call | tf_op jit(solution)/shard_map/far_field/pallas_call | solution.py:222
  (6 shorter events, 0.1 us)
Async XLA Ops:
  0.0 40.7 %copy-start = (bf16[8,256,256]{2,1,0:T(8,128)(2,1)S(1)}, bf16[8,256,256]{2,1,0:T(8,128)(2,1)}, u32[]{:S(2)}) copy-start(bf16[8,256,256]{2,1,0:T(8,128)(2,1)} %down_ref.1) | copy-start | bytes 3145732
  1.6 1.0 %copy-start.1 = (bf16[1024,256]{1,0:T(8,128)(2,1)S(1)}, bf16[1024,256]{1,0:T(8,128)(2,1)}, u32[]{:S(2)}) copy-start(bf16[1024,256]{1,0:T(8,128)(2,1)} %cells_ref.1) | copy-start | bytes 1572868
  5.1 35.6 %all-to-all-start = ((bf16[32,72,128]{2,1,0:T(8,128)(2,1)}), bf16[32,72,128]{2,1,0:T(8,128)(2,1)S(1)}, u32[]{:S(2)}, u32[]{:S(2)}) async-start(bf16[32,72,128]{2,1,0:T(8,128)(2,1)} %get-tuple-element.9), calls=%async_computation | async-start | bytes 1179648 | tf_op jit(solution)/shard_map/all_to_all | solution.py:200
  12.8 18.4 %collective-permute-start.2 = (bf16[64,128]{1,0:T(8,128)(2,1)S(1)}, bf16[64,128]{1,0:T(8,128)(2,1)S(1)}, u32[]{:S(2)}, u32[]{:S(2)}) collective-permute-start(bf16[64,128]{1,0:T(8,128)(2,1)S(1)} %get-tuple-element.13), channel_id=1, source_target_pairs={{16,0},{24,8},{32,16},{40,24},{48,32},{56,40},{64,48},{72,56},{80,... | collective-permute-start | bytes 49160 | tf_op jit(solution)/shard_map/ppermute | solution.py:207
  17.6 17.4 %collective-permute-start.5 = (bf16[64,128]{1,0:T(8,128)(2,1)S(1)}, bf16[64,128]{1,0:T(8,128)(2,1)S(1)}, u32[]{:S(2)}, u32[]{:S(2)}) collective-permute-start(bf16[64,128]{1,0:T(8,128)(2,1)S(1)} %get-tuple-element.14), channel_id=1, source_target_pairs={{0,16},{8,24},{16,32},{24,40},{32,48},{40,56},{48,64},{56,72},{64,... | collective-permute-start | bytes 49160 | tf_op jit(solution)/shard_map/ppermute | solution.py:207
  19.6 15.5 %collective-permute-start.4 = (bf16[64,128]{1,0:T(8,128)(2,1)S(1)}, bf16[64,128]{1,0:T(8,128)(2,1)S(1)}, u32[]{:S(2)}, u32[]{:S(2)}) collective-permute-start(bf16[64,128]{1,0:T(8,128)(2,1)S(1)} %get-tuple-element.15), channel_id=1, source_target_pairs={{0,8},{8,16},{16,24},{24,32},{32,40},{40,48},{48,56},{56,64},{64,7... | collective-permute-start | bytes 49160 | tf_op jit(solution)/shard_map/ppermute | solution.py:207
  21.5 13.6 %collective-permute-start.3 = (bf16[64,128]{1,0:T(8,128)(2,1)S(1)}, bf16[64,128]{1,0:T(8,128)(2,1)S(1)}, u32[]{:S(2)}, u32[]{:S(2)}) collective-permute-start(bf16[64,128]{1,0:T(8,128)(2,1)S(1)} %get-tuple-element.16), channel_id=1, source_target_pairs={{8,0},{16,8},{24,16},{32,24},{40,32},{48,40},{56,48},{64,56},{72,6... | collective-permute-start | bytes 49160 | tf_op jit(solution)/shard_map/ppermute | solution.py:207
  27.3 8.3 %collective-permute-start.1 = (bf16[1024,128]{1,0:T(8,128)(2,1)S(1)}, bf16[1024,128]{1,0:T(8,128)(2,1)S(1)}, u32[]{:S(2)}, u32[]{:S(2)}) collective-permute-start(bf16[1024,128]{1,0:T(8,128)(2,1)S(1)} %get-tuple-element.11), channel_id=1, source_target_pairs={{1,0},{2,1},{3,2},{4,3},{5,4},{6,5},{7,6},{9,8},{10,9},{11,10},{12... | collective-permute-start | bytes 786440 | tf_op jit(solution)/shard_map/ppermute | solution.py:205
  31.2 9.5 %collective-permute-start = (bf16[1024,128]{1,0:T(8,128)(2,1)S(1)}, bf16[1024,128]{1,0:T(8,128)(2,1)S(1)}, u32[]{:S(2)}, u32[]{:S(2)}) collective-permute-start(bf16[1024,128]{1,0:T(8,128)(2,1)S(1)} %get-tuple-element.12), channel_id=1, source_target_pairs={{0,1},{1,2},{2,3},{3,4},{4,5},{5,6},{6,7},{8,9},{9,10},{10,11},{11... | collective-permute-start | bytes 786440 | tf_op jit(solution)/shard_map/ppermute | solution.py:204

commit v2 on v1

v2 whole, which is shorter than its diff:
```python
import functools

import jax
import jax.numpy as jnp
from jax import lax
from jax.experimental import pallas as pl
from jax.experimental.pallas import tpu as pltpu
from jax.sharding import PartitionSpec as P

NEAR = (-2, -1, 1, 2)
FAR_SLOTS = 32
LANES = 128
TARGETS = 512
CLASSES = 16
SLOT_ROWS = 1024
WINDOW = 4096
BLANK = 2 * WINDOW
TOP_BASE = BLANK + 16


def split_rows(source, count, table, target, step=256):
    for first in range(0, count, step):
        wide = source[first : first + step, :].astype(jnp.float32)
        table[pl.ds(target + 2 * first, step, stride=2), :] = wide[:, :LANES]
        table[pl.ds(target + 2 * first + 1, step, stride=2), :] = wide[:, LANES:]


def send_kernel(
    peers, me_ref, pick_hbm, cells_hbm, top_hbm, out_ref, picks, cells, top, table, rows, sems
):
    copies = [
        pltpu.make_async_copy(source, target, sems.at[i])
        for i, (source, target) in enumerate(
            ((pick_hbm.at[0], picks), (cells_hbm, cells), (top_hbm, top))
        )
    ]
    for copy in copies:
        copy.start()
    tops = 2 * top.shape[0]
    slots = picks.shape[1]
    slab = 2 * slots
    pitch = slab + tops
    for first in range(0, rows.shape[0], pitch):
        rows[first : first + pitch, :] = jnp.zeros((pitch, LANES), jnp.float32)
    for copy in copies:
        copy.wait()
    split_rows(cells, cells.shape[0], table, 0)
    for half in range(2):
        part = top[:, half * LANES : (half + 1) * LANES]
        for peer in range(peers):
            rows[pl.ds(peer * pitch + slab + half, top.shape[0], stride=2), :] = part

    def pick(peer, slot, base):
        source = pl.multiple_of(2 * picks[peer, slot], 2)
        rows[pl.ds(pl.multiple_of(base + 2 * slot, 2), 2), :] = table[pl.ds(source, 2), :]

    for distance in NEAR:
        peer = jnp.clip(me_ref[0] + distance, 0, peers - 1)
        for slot in range(FAR_SLOTS, slots):
            pick(peer, slot, peer * pitch)
    for peer in range(peers):
        for slot in range(FAR_SLOTS):
            pick(peer, slot, peer * pitch)
        out_ref[peer] = rows[peer * pitch : (peer + 1) * pitch, :].astype(jnp.bfloat16)


def main_kernel(
    peers,
    index_ref,
    low_ref,
    own_ref,
    high_ref,
    incoming_ref,
    ops_ref,
    down_ref,
    out_ref,
    table,
    index_a,
    index_b,
    index_top,
    picked,
    total,
    index_sem,
):
    leaves = out_ref.shape[0]
    slots = ops_ref.shape[0]
    chunk = SLOT_ROWS
    per_block = TARGETS * slots // chunk
    steps = leaves * slots // chunk
    indices = (index_a, index_b)

    def fetch(step, slot):
        first = pl.multiple_of(step * chunk, chunk)
        return pltpu.make_async_copy(
            index_ref.at[pl.ds(first, chunk)], indices[slot], index_sem.at[slot]
        )

    top_fetch = pltpu.make_async_copy(
        index_ref.at[pl.ds(leaves * slots, leaves)], index_top, index_sem.at[2]
    )
    top_fetch.start()
    fetch(0, 0).start()
    fetch(1, 1).start()

    rim = 2 * low_ref.shape[0]
    own = 2 * own_ref.shape[0]
    split_rows(low_ref, low_ref.shape[0], table, 0)
    split_rows(own_ref, own_ref.shape[0], table, rim)
    split_rows(high_ref, high_ref.shape[0], table, rim + own)
    remote = 2 * rim + own
    per_peer = (BLANK - remote) // peers
    tops = incoming_ref.shape[1] - per_peer
    for peer in range(peers):
        part = incoming_ref[peer].astype(jnp.float32)
        table[remote + peer * per_peer : remote + (peer + 1) * per_peer, :] = part[:per_peer]
        table[TOP_BASE + peer * tops : TOP_BASE + (peer + 1) * tops, :] = part[per_peer:]
    table[BLANK:TOP_BASE, :] = jnp.zeros((TOP_BASE - BLANK, LANES), jnp.float32)
    def gather(where, position, base):
        source = pl.multiple_of(where[position], 2)
        target = pl.multiple_of(base + 2 * position, 2)
        picked[pl.ds(target, 2), :] = table[pl.ds(source, 2), :]

    def halves(rows, first, count):
        return [
            rows[pl.ds(2 * first + half, count, stride=2), :].astype(jnp.bfloat16)
            for half in range(2)
        ]

    top_fetch.wait()
    octants = down_ref.shape[0]
    share = leaves // octants
    for position in range(leaves):
        gather(index_top, position, 0)
    for octant in range(octants):
        lhs = jnp.concatenate(halves(picked, octant * share, share), axis=1)
        inherited = jnp.dot(lhs, down_ref[octant], preferred_element_type=jnp.float32)
        for half in range(2):
            total.at[half][pl.ds(octant, share, stride=octants), :] = inherited[
                :, half * LANES : (half + 1) * LANES
            ]

    def gather_step(step, base, slot):
        fetch(step, slot).wait()
        for row in range(chunk):
            gather(indices[slot], row, base)

        @pl.when(step + 2 < steps)
        def _():
            fetch(step + 2, slot).start()

    def block_step(block, carry):
        def pair(index, carry):
            base = pl.multiple_of(index * 4 * chunk, 4 * chunk)
            gather_step(block * per_block + 2 * index, base, 0)
            gather_step(block * per_block + 2 * index + 1, base + 2 * chunk, 1)
            return carry

        lax.fori_loop(0, per_block // 2, pair, 0)

        def multiply(group, carry):
            first = pl.multiple_of(group * CLASSES * TARGETS, CLASSES * TARGETS)
            lhs = jnp.concatenate(
                [
                    x
                    for member in range(CLASSES)
                    for x in halves(picked, first + member * TARGETS, TARGETS)
                ],
                axis=1,
            )
            rhs = ops_ref[pl.ds(group * CLASSES, CLASSES)]
            rhs = rhs.reshape(CLASSES * 2 * LANES, 2 * LANES)
            product = jnp.dot(lhs, rhs, preferred_element_type=jnp.float32)
            rows = pl.ds(pl.multiple_of(block * TARGETS, TARGETS), TARGETS)
            for half in range(2):
                total[half, rows, :] += product[:, half * LANES : (half + 1) * LANES]
            return carry

        lax.fori_loop(0, slots // CLASSES, multiply, 0)
        return carry

    lax.fori_loop(0, leaves // TARGETS, block_step, 0)
    for half in range(2):
        out_ref[:, half * LANES : (half + 1) * LANES] = total[half]


def on_device(multipoles, send_rows, send_count, lists, operators, top_local, ancestor, down_ops):
    leaves, coefs = multipoles.shape
    slots = operators.shape[0]
    peers = lax.axis_size("morton")
    me = lax.axis_index("morton")
    tops = 2 * top_local.shape[0]
    pitch = 2 * send_rows.shape[2] + tops
    total_rows = peers * pitch
    vmem = pl.BlockSpec(memory_space=pltpu.VMEM)
    smem = pl.BlockSpec(memory_space=pltpu.SMEM)
    hbm = pl.BlockSpec(memory_space=pltpu.HBM)
    outgoing = pl.pallas_call(
        functools.partial(send_kernel, peers),
        out_shape=jax.ShapeDtypeStruct((peers, pitch, LANES), jnp.bfloat16),
        in_specs=[smem, hbm, hbm, hbm],
        out_specs=vmem,
        scratch_shapes=[
            pltpu.SMEM(send_rows.shape[1:], jnp.int32),
            pltpu.VMEM(multipoles.shape, jnp.bfloat16),
            pltpu.VMEM(top_local.shape, jnp.float32),
            pltpu.VMEM((2 * leaves, LANES), jnp.float32),
            pltpu.VMEM((total_rows, LANES), jnp.float32),
            pltpu.SemaphoreType.DMA((3,)),
        ],
        compiler_params=pltpu.CompilerParams(vmem_limit_bytes=60 * 2**20),
        name="send_rows",
    )(me[None], send_rows, multipoles, top_local)
    incoming = lax.all_to_all(outgoing, "morton", split_axis=0, concat_axis=0, tiled=True)
    ranks = lax.axis_size("coef")
    forward = [(i, i + 1) for i in range(ranks - 1)]
    backward = [(i + 1, i) for i in range(ranks - 1)]
    low = lax.ppermute(multipoles[leaves // 2 :], "coef", forward)
    high = lax.ppermute(multipoles[: leaves // 2], "coef", backward)
    entries = jnp.where(lists >= 0, 2 * lists, BLANK).T
    entries = entries.reshape(slots, leaves // TARGETS, TARGETS).transpose(1, 0, 2).reshape(-1)
    octants = down_ops.shape[0]
    parents = (TOP_BASE + 2 * ancestor).reshape(leaves // octants, octants).T.reshape(-1)
    index = jnp.concatenate([entries, parents])
    chunk = SLOT_ROWS
    return pl.pallas_call(
        functools.partial(main_kernel, peers),
        out_shape=jax.ShapeDtypeStruct((leaves, coefs), jnp.float32),
        in_specs=[vmem] * 7,
        out_specs=vmem,
        scratch_shapes=[
            pltpu.VMEM((TOP_BASE + peers * tops, LANES), jnp.float32),
            pltpu.SMEM((chunk,), jnp.int32),
            pltpu.SMEM((chunk,), jnp.int32),
            pltpu.SMEM((leaves,), jnp.int32),
            pltpu.VMEM((2 * TARGETS * slots, LANES), jnp.float32),
            pltpu.VMEM((2, leaves, LANES), jnp.float32),
            pltpu.SemaphoreType.DMA((3,)),
        ],
        compiler_params=pltpu.CompilerParams(vmem_limit_bytes=48 * 2**20),
        name="far_field",
    )(index, low, multipoles, high, incoming, operators, down_ops)


def solution(mesh):
    placed = (
        P(("morton", "coef"), None),
        P(("morton", "coef"), None, None),
        P(("morton", "coef"), None),
        P(("morton", "coef"), None),
        P(),
        P("morton", None),
        P(("morton", "coef")),
        P(),
    )
    return jax.shard_map(
        on_device,
        mesh=mesh,
        in_specs=placed,
        out_specs=P(("morton", "coef"), None),
        check_vma=False,
    )
```

time: 72.5 us -> 58 us (0.80)
  the two profiles are of different devices: /device:TPU:134 before, /device:TPU:1 now
where the time goes in v2:
time: 58 us; the launch traced here: 57.7 us
  Pallas kernels  31.3 us (54%)
  starting transfers between devices  13.6 us (23%)
  waiting for transfers between devices  11.6 us (20%)
  local copies, waits for them, and re-layouts  1.04 us (2%)
    pallas_call x1, Pallas kernels, on_device(): pl.pallas_call(functools.partial(main_kernel, peers), out_shape=jax.Shape...  28 us
    all_to_all x1, starting transfers between devices, on_device(): lax.all_to_all(outgoing, 'morton', split_axis=0, concat_axis=0, tiled=True)  8.73 us
    ppermute x1, waiting for transfers between devices, on_device(): low = lax.ppermute(multipoles[leaves // 2:], 'coef', forward)  4.16 us
    ppermute x1, waiting for transfers between devices, on_device(): high = lax.ppermute(multipoles[:leaves // 2], 'coef', backward)  4.07 us
    ppermute x1, starting transfers between devices, on_device(): low = lax.ppermute(multipoles[leaves // 2:], 'coef', forward)  3.54 us
    all_to_all x1, waiting for transfers between devices, on_device(): lax.all_to_all(outgoing, 'morton', split_axis=0, concat_axis=0, tiled=True)  3.39 us
    pallas_call x1, Pallas kernels, on_device(): pl.pallas_call(functools.partial(send_kernel, peers), out_shape=jax.Shape...  3.34 us
    ppermute x1, starting transfers between devices, on_device(): high = lax.ppermute(multipoles[:leaves // 2], 'coef', backward)  1.29 us
  transfers between devices with their start and end apart: 3, of which 3 were waited for; matrix products, arithmetic and copies ran while one was open for 2% of the time, Pallas kernels for 0%

profile of v2, /device:TPU:1, one launch (start us, length us, event | category | flops | bytes accessed | tf_op | source)
XLA Modules:
  0.0 57.7 jit_solution(15283971278288163750)
XLA Ops:
  0.0 3.3 %send_rows.1 = bf16[32,136,128]{2,1,0:T(8,128)(2,1)} custom-call(s32[1]{0:T(128)} %bitcast.4.me_ref, s32[1,32,64]{2,1,0:T(8,128)} %pick_hbm.1, bf16[1024,256]{1,0:T(8,128)(2,1)} %own_ref.1, f32[4,256]{1,0:T(4,128)} %top_hbm.1), custom_call_target="tpu_custom_call" | custom-call | tf_op jit(solution)/shard_map/send_rows/pallas_call | solution.py:197
  3.4 0.0 copy-start
  3.4 0.0 copy-start.2
  3.4 8.7 %all-to-all-start = ((bf16[32,136,128]{2,1,0:T(8,128)(2,1)}), bf16[32,136,128]{2,1,0:T(8,128)(2,1)S(1)}, u32[]{:S(2)}, u32[]{:S(2)}) async-start(bf16[32,136,128]{2,1,0:T(8,128)(2,1)} %send_rows.1), calls=%async_computation | async-start | bytes 2228224 | tf_op jit(solution)/shard_map/all_to_all | solution.py:213
  12.1 0.0 copy-done
  12.1 0.0 copy-start.3
  12.1 0.0 copy-start.1
  12.1 0.8 %fusion = (bf16[512,256]{1,0:T(8,128)(2,1)}, bf16[512,256]{1,0:T(8,128)(2,1)}) fusion(bf16[1024,256]{1,0:T(8,128)(2,1)S(1)} %copy-done), kind=kLoop, calls=%fused_computation.4 | loop fusion | bytes 1048576 | tf_op jit(solution)/shard_map/slice | solution.py:218
  13.0 3.5 %collective-permute-start = (bf16[512,256]{1,0:T(8,128)(2,1)}, bf16[512,256]{1,0:T(8,128)(2,1)S(1)}, u32[]{:S(2)}, u32[]{:S(2)}) collective-permute-start(bf16[512,256]{1,0:T(8,128)(2,1)} %get-tuple-element.6), channel_id=1, source_target_pairs={{0,1},{1,2},{2,3},{3,4},{4,5},{5,6},{6,7},{8,9},{9,10},{10,11},{11... | collective-permute-start | bytes 786440 | tf_op jit(solution)/shard_map/ppermute | solution.py:217
  16.5 1.3 %collective-permute-start.1 = (bf16[512,256]{1,0:T(8,128)(2,1)}, bf16[512,256]{1,0:T(8,128)(2,1)S(1)}, u32[]{:S(2)}, u32[]{:S(2)}) collective-permute-start(bf16[512,256]{1,0:T(8,128)(2,1)} %get-tuple-element.5), channel_id=1, source_target_pairs={{1,0},{2,1},{3,2},{4,3},{5,4},{6,5},{7,6},{9,8},{10,9},{11,10},{12... | collective-permute-start | bytes 786440 | tf_op jit(solution)/shard_map/ppermute | solution.py:218
  17.8 0.0 copy-done.2
  17.9 0.0 copy-done.3
  18.0 0.1 reshape.14
  18.1 4.2 %collective-permute-done.low_ref = bf16[512,256]{1,0:T(8,128)(2,1)S(1)} collective-permute-done((bf16[512,256]{1,0:T(8,128)(2,1)}, bf16[512,256]{1,0:T(8,128)(2,1)S(1)}, u32[]{:S(2)}, u32[]{:S(2)}) %collective-permute-start) | collective-permute-done | bytes 262176 | tf_op jit(solution)/shard_map/ppermute | solution.py:217
  22.3 4.1 %collective-permute-done.1.high_ref = bf16[512,256]{1,0:T(8,128)(2,1)S(1)} collective-permute-done((bf16[512,256]{1,0:T(8,128)(2,1)}, bf16[512,256]{1,0:T(8,128)(2,1)S(1)}, u32[]{:S(2)}, u32[]{:S(2)}) %collective-permute-start.1) | collective-permute-done | bytes 262176 | tf_op jit(solution)/shard_map/ppermute | solution.py:218
  26.4 3.4 %all-to-all-done.incoming_ref = bf16[32,136,128]{2,1,0:T(8,128)(2,1)S(1)} async-done(((bf16[32,136,128]{2,1,0:T(8,128)(2,1)}), bf16[32,136,128]{2,1,0:T(8,128)(2,1)S(1)}, u32[]{:S(2)}, u32[]{:S(2)}) %all-to-all-start) | async-done | bytes 1114144 | tf_op jit(solution)/shard_map/all_to_all | solution.py:213
  29.8 0.0 copy-done.1
  29.8 28.0 %far_field.1 = f32[1024,256]{1,0:T(8,128)} custom-call(s32[33792]{0:T(1024)S(1)} %pad_add_fusion.index_ref, bf16[512,256]{1,0:T(8,128)(2,1)S(1)} %collective-permute-done.low_ref, bf16[1024,256]{1,0:T(8,128)(2,1)S(1)} %copy-done, bf16[512,256]{1,0:T(8,128)(2,1)S(1)} %collective-permute-done.1.high_ref, bf16[32,136,128]{2,1,0:T(8,128)(2,1)S(1)} %all-to-all-done.incoming_ref, ...), custom_call_target="tpu_custom_call" | custom-call | tf_op jit(solution)/shard_map/far_field/pallas_call | solution.py:225
  (6 shorter events, 0.1 us)
Async XLA Ops:
  3.4 8.8 %copy-start = (bf16[1024,256]{1,0:T(8,128)(2,1)S(1)}, bf16[1024,256]{1,0:T(8,128)(2,1)}, u32[]{:S(2)}) copy-start(bf16[1024,256]{1,0:T(8,128)(2,1)} %own_ref.1) | copy-start | bytes 1572868
  3.4 14.5 %copy-start.2 = (s32[1024,32]{0,1:T(8,128)S(1)}, s32[1024,32]{0,1:T(8,128)}, u32[]{:S(2)}) copy-start(s32[1024,32]{0,1:T(8,128)} %param.10) | copy-start | bytes 393220
  3.4 26.4 %all-to-all-start = ((bf16[32,136,128]{2,1,0:T(8,128)(2,1)}), bf16[32,136,128]{2,1,0:T(8,128)(2,1)S(1)}, u32[]{:S(2)}, u32[]{:S(2)}) async-start(bf16[32,136,128]{2,1,0:T(8,128)(2,1)} %send_rows.1), calls=%async_computation | async-start | bytes 2228224 | tf_op jit(solution)/shard_map/all_to_all | solution.py:213
  12.1 5.8 %copy-start.3 = (s32[1024]{0:T(1024)S(1)}, s32[1024]{0:T(1024)}, u32[]{:S(2)}) copy-start(s32[1024]{0:T(1024)} %param.13) | copy-start | bytes 12292
  12.1 17.6 %copy-start.1 = (bf16[8,256,256]{2,1,0:T(8,128)(2,1)S(1)}, bf16[8,256,256]{2,1,0:T(8,128)(2,1)}, u32[]{:S(2)}) copy-start(bf16[8,256,256]{2,1,0:T(8,128)(2,1)} %down_ref.1) | copy-start | bytes 3145732
  13.0 9.3 %collective-permute-start = (bf16[512,256]{1,0:T(8,128)(2,1)}, bf16[512,256]{1,0:T(8,128)(2,1)S(1)}, u32[]{:S(2)}, u32[]{:S(2)}) collective-permute-start(bf16[512,256]{1,0:T(8,128)(2,1)} %get-tuple-element.6), channel_id=1, source_target_pairs={{0,1},{1,2},{2,3},{3,4},{4,5},{5,6},{6,7},{8,9},{9,10},{10,11},{11... | collective-permute-start | bytes 786440 | tf_op jit(solution)/shard_map/ppermute | solution.py:217
  16.5 9.8 %collective-permute-start.1 = (bf16[512,256]{1,0:T(8,128)(2,1)}, bf16[512,256]{1,0:T(8,128)(2,1)S(1)}, u32[]{:S(2)}, u32[]{:S(2)}) collective-permute-start(bf16[512,256]{1,0:T(8,128)(2,1)} %get-tuple-element.5), channel_id=1, source_target_pairs={{1,0},{2,1},{3,2},{4,3},{5,4},{6,5},{7,6},{9,8},{10,9},{11,10},{12... | collective-permute-start | bytes 786440 | tf_op jit(solution)/shard_map/ppermute | solution.py:218

commit v3 on v2

--- a/solution.py
+++ b/solution.py
@@ -11,11 +11,10 @@
 FAR_SLOTS = 32
 LANES = 128
 TARGETS = 512
-CLASSES = 16
+CLASSES = 32
 SLOT_ROWS = 1024
 WINDOW = 4096
 BLANK = 2 * WINDOW
-TOP_BASE = BLANK + 16
 
 
 def split_rows(source, count, table, target, step=256):
@@ -42,13 +41,15 @@
     pitch = slab + tops
     for first in range(0, rows.shape[0], pitch):
         rows[first : first + pitch, :] = jnp.zeros((pitch, LANES), jnp.float32)
-    for copy in copies:
-        copy.wait()
+    copies[0].wait()
+    copies[1].wait()
     split_rows(cells, cells.shape[0], table, 0)
+    copies[2].wait()
     for half in range(2):
         part = top[:, half * LANES : (half + 1) * LANES]
         for peer in range(peers):
             rows[pl.ds(peer * pitch + slab + half, top.shape[0], stride=2), :] = part
+
 
     def pick(peer, slot, base):
         source = pl.multiple_of(2 * picks[peer, slot], 2)
@@ -67,22 +68,28 @@
 def main_kernel(
     peers,
     index_ref,
+    parent_ref,
     low_ref,
     own_ref,
     high_ref,
     incoming_ref,
-    ops_ref,
-    down_ref,
-    out_ref,
+    ops_hbm,
+    down_hbm,
+    out_hbm,
     table,
     index_a,
     index_b,
-    index_top,
+    top_table,
     picked,
     total,
+    ops_ref,
+    down_ref,
+    staged,
     index_sem,
+    weight_sem,
+    out_sem,
 ):
-    leaves = out_ref.shape[0]
+    leaves = out_hbm.shape[0]
     slots = ops_ref.shape[0]
     chunk = SLOT_ROWS
     per_block = TARGETS * slots // chunk
@@ -95,12 +102,14 @@
             index_ref.at[pl.ds(first, chunk)], indices[slot], index_sem.at[slot]
         )
 
-    top_fetch = pltpu.make_async_copy(
-        index_ref.at[pl.ds(leaves * slots, leaves)], index_top, index_sem.at[2]
-    )
-    top_fetch.start()
+    weights = [
+        pltpu.make_async_copy(source, target, weight_sem.at[i])
+        for i, (source, target) in enumerate(((down_hbm, down_ref), (ops_hbm, ops_ref)))
+    ]
     fetch(0, 0).start()
     fetch(1, 1).start()
+    for weight in weights:
+        weight.start()
 
     rim = 2 * low_ref.shape[0]
     own = 2 * own_ref.shape[0]
@@ -113,8 +122,8 @@
     for peer in range(peers):
         part = incoming_ref[peer].astype(jnp.float32)
         table[remote + peer * per_peer : remote + (peer + 1) * per_peer, :] = part[:per_peer]
-        table[TOP_BASE + peer * tops : TOP_BASE + (peer + 1) * tops, :] = part[per_peer:]
-    table[BLANK:TOP_BASE, :] = jnp.zeros((TOP_BASE - BLANK, LANES), jnp.float32)
+        top_table[peer * tops : (peer + 1) * tops, :] = part[per_peer:]
+    table[BLANK:, :] = jnp.zeros((table.shape[0] - BLANK, LANES), jnp.float32)
     def gather(where, position, base):
         source = pl.multiple_of(where[position], 2)
         target = pl.multiple_of(base + 2 * position, 2)
@@ -126,14 +135,27 @@
             for half in range(2)
         ]
 
-    top_fetch.wait()
+    weights[0].wait()
     octants = down_ref.shape[0]
     share = leaves // octants
-    for position in range(leaves):
-        gather(index_top, position, 0)
+    top_count = top_table.shape[0] // 2
+    top_rows = jnp.concatenate(
+        [
+            top_table[pl.ds(half, top_count, stride=2), :].astype(jnp.bfloat16)
+            for half in range(2)
+        ],
+        axis=1,
+    )
+    top_ids = lax.broadcasted_iota(jnp.int32, (top_count, share), 0)
     for octant in range(octants):
-        lhs = jnp.concatenate(halves(picked, octant * share, share), axis=1)
-        inherited = jnp.dot(lhs, down_ref[octant], preferred_element_type=jnp.float32)
+        chosen = jnp.where(top_ids == parent_ref[octant : octant + 1, :], 1.0, 0.0)
+        lifted = lax.dot_general(
+            chosen.astype(jnp.bfloat16),
+            top_rows,
+            (((0,), (0,)), ((), ())),
+            preferred_element_type=jnp.float32,
+        ).astype(jnp.bfloat16)
+        inherited = jnp.dot(lifted, down_ref[octant], preferred_element_type=jnp.float32)
         for half in range(2):
             total.at[half][pl.ds(octant, share, stride=octants), :] = inherited[
                 :, half * LANES : (half + 1) * LANES
@@ -147,6 +169,10 @@
         @pl.when(step + 2 < steps)
         def _():
             fetch(step + 2, slot).start()
+
+    def send_out(block):
+        rows = pl.ds(pl.multiple_of(block * TARGETS, TARGETS), TARGETS)
+        return pltpu.make_async_copy(staged.at[rows], out_hbm.at[rows], out_sem.at[block])
 
     def block_step(block, carry):
         def pair(index, carry):
@@ -156,6 +182,10 @@
             return carry
 
         lax.fori_loop(0, per_block // 2, pair, 0)
+
+        @pl.when(block == 0)
+        def _():
+            weights[1].wait()
 
         def multiply(group, carry):
             first = pl.multiple_of(group * CLASSES * TARGETS, CLASSES * TARGETS)
@@ -176,11 +206,15 @@
             return carry
 
         lax.fori_loop(0, slots // CLASSES, multiply, 0)
+        rows = pl.ds(pl.multiple_of(block * TARGETS, TARGETS), TARGETS)
+        for half in range(2):
+            staged[rows, half * LANES : (half + 1) * LANES] = total[half, rows, :]
+        send_out(block).start()
         return carry
 
     lax.fori_loop(0, leaves // TARGETS, block_step, 0)
-    for half in range(2):
-        out_ref[:, half * LANES : (half + 1) * LANES] = total[half]
+    for block in range(leaves // TARGETS):
+        send_out(block).wait()
 
 
 def on_device(multipoles, send_rows, send_count, lists, operators, top_local, ancestor, down_ops):
@@ -219,26 +253,30 @@
     entries = jnp.where(lists >= 0, 2 * lists, BLANK).T
     entries = entries.reshape(slots, leaves // TARGETS, TARGETS).transpose(1, 0, 2).reshape(-1)
     octants = down_ops.shape[0]
-    parents = (TOP_BASE + 2 * ancestor).reshape(leaves // octants, octants).T.reshape(-1)
-    index = jnp.concatenate([entries, parents])
+    parents = ancestor.reshape(leaves // octants, octants).T
     chunk = SLOT_ROWS
     return pl.pallas_call(
         functools.partial(main_kernel, peers),
         out_shape=jax.ShapeDtypeStruct((leaves, coefs), jnp.float32),
-        in_specs=[vmem] * 7,
-        out_specs=vmem,
+        in_specs=[vmem] * 6 + [hbm] * 2,
+        out_specs=hbm,
         scratch_shapes=[
-            pltpu.VMEM((TOP_BASE + peers * tops, LANES), jnp.float32),
+            pltpu.VMEM((BLANK + 16, LANES), jnp.float32),
             pltpu.SMEM((chunk,), jnp.int32),
             pltpu.SMEM((chunk,), jnp.int32),
-            pltpu.SMEM((leaves,), jnp.int32),
+            pltpu.VMEM((peers * tops, LANES), jnp.float32),
             pltpu.VMEM((2 * TARGETS * slots, LANES), jnp.float32),
             pltpu.VMEM((2, leaves, LANES), jnp.float32),
-            pltpu.SemaphoreType.DMA((3,)),
+            pltpu.VMEM(operators.shape, operators.dtype),
+            pltpu.VMEM(down_ops.shape, down_ops.dtype),
+            pltpu.VMEM((leaves, coefs), jnp.float32),
+            pltpu.SemaphoreType.DMA((2,)),
+            pltpu.SemaphoreType.DMA((2,)),
+            pltpu.SemaphoreType.DMA((leaves // TARGETS,)),
         ],
         compiler_params=pltpu.CompilerParams(vmem_limit_bytes=48 * 2**20),
         name="far_field",
-    )(index, low, multipoles, high, incoming, operators, down_ops)
+    )(entries, parents, low, multipoles, high, incoming, operators, down_ops)
 
 
 def solution(mesh):

time: 58 us -> 54.6 us (0.941)
  Pallas kernels: 31.3 us -> 27.9 us
    pallas_call x1, Pallas kernels: 28 us -> 24.6 us  [on_device(): pl.pallas_call(functools.partial(main_kernel, peers), out_shape=jax.Shape...]
where the time goes in v3:
time: 54.6 us; the launch traced here: 54.4 us
  Pallas kernels  27.9 us (51%)
  starting transfers between devices  13.6 us (25%)
  waiting for transfers between devices  11.7 us (21%)
  local copies, waits for them, and re-layouts  1.04 us (2%)
    pallas_call x1, Pallas kernels, on_device(): pl.pallas_call(functools.partial(main_kernel, peers), out_shape=jax.Shape...  24.6 us
    all_to_all x1, starting transfers between devices, on_device(): lax.all_to_all(outgoing, 'morton', split_axis=0, concat_axis=0, tiled=True)  8.73 us
    ppermute x1, waiting for transfers between devices, on_device(): low = lax.ppermute(multipoles[leaves // 2:], 'coef', forward)  4.21 us
    ppermute x1, waiting for transfers between devices, on_device(): high = lax.ppermute(multipoles[:leaves // 2], 'coef', backward)  4.07 us
    ppermute x1, starting transfers between devices, on_device(): low = lax.ppermute(multipoles[leaves // 2:], 'coef', forward)  3.55 us
    all_to_all x1, waiting for transfers between devices, on_device(): lax.all_to_all(outgoing, 'morton', split_axis=0, concat_axis=0, tiled=True)  3.39 us
    pallas_call x1, Pallas kernels, on_device(): pl.pallas_call(functools.partial(send_kernel, peers), out_shape=jax.Shape...  3.36 us
    ppermute x1, starting transfers between devices, on_device(): high = lax.ppermute(multipoles[:leaves // 2], 'coef', backward)  1.29 us
  transfers between devices with their start and end apart: 3, of which 3 were waited for; matrix products, arithmetic and copies ran while one was open for 2% of the time, Pallas kernels for 0%

profile of v3, /device:TPU:1, one launch (start us, length us, event | category | flops | bytes accessed | tf_op | source)
XLA Modules:
  0.0 54.4 jit_solution(3908139479563195207)
XLA Ops:
  0.0 3.4 %send_rows.1 = bf16[32,136,128]{2,1,0:T(8,128)(2,1)} custom-call(s32[1]{0:T(128)} %bitcast.3.me_ref, s32[1,32,64]{2,1,0:T(8,128)} %pick_hbm.1, bf16[1024,256]{1,0:T(8,128)(2,1)} %own_ref.1, f32[4,256]{1,0:T(4,128)} %top_hbm.1), custom_call_target="tpu_custom_call" | custom-call | tf_op jit(solution)/shard_map/send_rows/pallas_call | solution.py:231
  3.4 0.0 copy-start
  3.4 0.0 copy-start.2
  3.4 8.7 %all-to-all-start = ((bf16[32,136,128]{2,1,0:T(8,128)(2,1)}), bf16[32,136,128]{2,1,0:T(8,128)(2,1)S(1)}, u32[]{:S(2)}, u32[]{:S(2)}) async-start(bf16[32,136,128]{2,1,0:T(8,128)(2,1)} %send_rows.1), calls=%async_computation | async-start | bytes 2228224 | tf_op jit(solution)/shard_map/all_to_all | solution.py:247
  12.1 0.0 copy-done
  12.1 0.0 copy-start.3
  12.2 0.0 copy-start.1
  12.2 0.8 %fusion = (bf16[512,256]{1,0:T(8,128)(2,1)}, bf16[512,256]{1,0:T(8,128)(2,1)}) fusion(bf16[1024,256]{1,0:T(8,128)(2,1)S(1)} %copy-done), kind=kLoop, calls=%fused_computation.2 | loop fusion | bytes 1048576 | tf_op jit(solution)/shard_map/slice | solution.py:252
  13.0 3.5 %collective-permute-start = (bf16[512,256]{1,0:T(8,128)(2,1)}, bf16[512,256]{1,0:T(8,128)(2,1)S(1)}, u32[]{:S(2)}, u32[]{:S(2)}) collective-permute-start(bf16[512,256]{1,0:T(8,128)(2,1)} %get-tuple-element.6), channel_id=1, source_target_pairs={{0,1},{1,2},{2,3},{3,4},{4,5},{5,6},{6,7},{8,9},{9,10},{10,11},{11... | collective-permute-start | bytes 786440 | tf_op jit(solution)/shard_map/ppermute | solution.py:251
  16.6 1.3 %collective-permute-start.1 = (bf16[512,256]{1,0:T(8,128)(2,1)}, bf16[512,256]{1,0:T(8,128)(2,1)S(1)}, u32[]{:S(2)}, u32[]{:S(2)}) collective-permute-start(bf16[512,256]{1,0:T(8,128)(2,1)} %get-tuple-element.5), channel_id=1, source_target_pairs={{1,0},{2,1},{3,2},{4,3},{5,4},{6,5},{7,6},{9,8},{10,9},{11,10},{12... | collective-permute-start | bytes 786440 | tf_op jit(solution)/shard_map/ppermute | solution.py:252
  17.9 0.0 copy-done.2
  18.0 0.0 copy-done.3
  18.0 0.1 reshape.11
  18.1 4.2 %collective-permute-done.low_ref = bf16[512,256]{1,0:T(8,128)(2,1)S(1)} collective-permute-done((bf16[512,256]{1,0:T(8,128)(2,1)}, bf16[512,256]{1,0:T(8,128)(2,1)S(1)}, u32[]{:S(2)}, u32[]{:S(2)}) %collective-permute-start) | collective-permute-done | bytes 262176 | tf_op jit(solution)/shard_map/ppermute | solution.py:251
  22.3 4.1 %collective-permute-done.1.high_ref = bf16[512,256]{1,0:T(8,128)(2,1)S(1)} collective-permute-done((bf16[512,256]{1,0:T(8,128)(2,1)}, bf16[512,256]{1,0:T(8,128)(2,1)S(1)}, u32[]{:S(2)}, u32[]{:S(2)}) %collective-permute-start.1) | collective-permute-done | bytes 262176 | tf_op jit(solution)/shard_map/ppermute | solution.py:252
  26.4 3.4 %all-to-all-done.incoming_ref = bf16[32,136,128]{2,1,0:T(8,128)(2,1)S(1)} async-done(((bf16[32,136,128]{2,1,0:T(8,128)(2,1)}), bf16[32,136,128]{2,1,0:T(8,128)(2,1)S(1)}, u32[]{:S(2)}, u32[]{:S(2)}) %all-to-all-start) | async-done | bytes 1114144 | tf_op jit(solution)/shard_map/all_to_all | solution.py:247
  29.8 0.0 copy-done.1
  29.8 24.6 %far_field.1 = f32[1024,256]{1,0:T(8,128)} custom-call(s32[32768]{0:T(1024)S(1)} %bitcast.10, s32[8,128]{1,0:T(8,128)S(1)} %bitcast.11, bf16[512,256]{1,0:T(8,128)(2,1)S(1)} %collective-permute-done.low_ref, bf16[1024,256]{1,0:T(8,128)(2,1)S(1)} %copy-done, bf16[512,256]{1,0:T(8,128)(2,1)S(1)} %collective-permute-done.1.high_ref, ...), custom_call_target="tpu_custom_call" | custom-call | tf_op jit(solution)/shard_map/far_field/pallas_call | solution.py:258
  (4 shorter events, 0.1 us)
Async XLA Ops:
  3.4 8.8 %copy-start = (bf16[1024,256]{1,0:T(8,128)(2,1)S(1)}, bf16[1024,256]{1,0:T(8,128)(2,1)}, u32[]{:S(2)}) copy-start(bf16[1024,256]{1,0:T(8,128)(2,1)} %own_ref.1) | copy-start | bytes 1572868
  3.4 14.5 %copy-start.2 = (s32[1024,32]{0,1:T(8,128)S(1)}, s32[1024,32]{0,1:T(8,128)}, u32[]{:S(2)}) copy-start(s32[1024,32]{0,1:T(8,128)} %param.10) | copy-start | bytes 393220
  3.4 26.4 %all-to-all-start = ((bf16[32,136,128]{2,1,0:T(8,128)(2,1)}), bf16[32,136,128]{2,1,0:T(8,128)(2,1)S(1)}, u32[]{:S(2)}, u32[]{:S(2)}) async-start(bf16[32,136,128]{2,1,0:T(8,128)(2,1)} %send_rows.1), calls=%async_computation | async-start | bytes 2228224 | tf_op jit(solution)/shard_map/all_to_all | solution.py:247
  12.1 5.8 %copy-start.3 = (s32[1024]{0:T(1024)S(1)}, s32[1024]{0:T(1024)}, u32[]{:S(2)}) copy-start(s32[1024]{0:T(1024)} %param.13) | copy-start | bytes 12292
  12.2 17.6 %copy-start.1 = (bf16[8,256,256]{2,1,0:T(8,128)(2,1)S(1)}, bf16[8,256,256]{2,1,0:T(8,128)(2,1)}, u32[]{:S(2)}) copy-start(bf16[8,256,256]{2,1,0:T(8,128)(2,1)} %down_hbm.1) | copy-start | bytes 3145732
  13.0 9.3 %collective-permute-start = (bf16[512,256]{1,0:T(8,128)(2,1)}, bf16[512,256]{1,0:T(8,128)(2,1)S(1)}, u32[]{:S(2)}, u32[]{:S(2)}) collective-permute-start(bf16[512,256]{1,0:T(8,128)(2,1)} %get-tuple-element.6), channel_id=1, source_target_pairs={{0,1},{1,2},{2,3},{3,4},{4,5},{5,6},{6,7},{8,9},{9,10},{10,11},{11... | collective-permute-start | bytes 786440 | tf_op jit(solution)/shard_map/ppermute | solution.py:251
  16.6 9.8 %collective-permute-start.1 = (bf16[512,256]{1,0:T(8,128)(2,1)}, bf16[512,256]{1,0:T(8,128)(2,1)S(1)}, u32[]{:S(2)}, u32[]{:S(2)}) collective-permute-start(bf16[512,256]{1,0:T(8,128)(2,1)} %get-tuple-element.5), channel_id=1, source_target_pairs={{1,0},{2,1},{3,2},{4,3},{5,4},{6,5},{7,6},{9,8},{10,9},{11,10},{12... | collective-permute-start | bytes 786440 | tf_op jit(solution)/shard_map/ppermute | solution.py:252

commit v4 on v3

--- a/solution.py
+++ b/solution.py
@@ -9,6 +9,7 @@
 
 NEAR = (-2, -1, 1, 2)
 FAR_SLOTS = 32
+PEER_GROUP = 8
 LANES = 128
 TARGETS = 512
 CLASSES = 32
@@ -25,7 +26,7 @@
 
 
 def send_kernel(
-    peers, me_ref, pick_hbm, cells_hbm, top_hbm, out_ref, picks, cells, top, table, rows, sems
+    peers, me_ref, pick_hbm, cells_hbm, top_hbm, out_hbm, picks, cells, top, table, rows, packed, sems, out_sems
 ):
     copies = [
         pltpu.make_async_copy(source, target, sems.at[i])
@@ -51,6 +52,10 @@
             rows[pl.ds(peer * pitch + slab + half, top.shape[0], stride=2), :] = part
 
 
+    def send_group(group):
+        part = pl.ds(group * PEER_GROUP, PEER_GROUP)
+        return pltpu.make_async_copy(packed.at[part], out_hbm.at[part], out_sems.at[group])
+
     def pick(peer, slot, base):
         source = pl.multiple_of(2 * picks[peer, slot], 2)
         rows[pl.ds(pl.multiple_of(base + 2 * slot, 2), 2), :] = table[pl.ds(source, 2), :]
@@ -62,7 +67,11 @@
     for peer in range(peers):
         for slot in range(FAR_SLOTS):
             pick(peer, slot, peer * pitch)
-        out_ref[peer] = rows[peer * pitch : (peer + 1) * pitch, :].astype(jnp.bfloat16)
+        packed[peer] = rows[peer * pitch : (peer + 1) * pitch, :].astype(jnp.bfloat16)
+        if peer % PEER_GROUP == PEER_GROUP - 1:
+            send_group(peer // PEER_GROUP).start()
+    for group in range(peers // PEER_GROUP):
+        send_group(group).wait()
 
 
 def main_kernel(
@@ -232,14 +241,16 @@
         functools.partial(send_kernel, peers),
         out_shape=jax.ShapeDtypeStruct((peers, pitch, LANES), jnp.bfloat16),
         in_specs=[smem, hbm, hbm, hbm],
-        out_specs=vmem,
+        out_specs=hbm,
         scratch_shapes=[
             pltpu.SMEM(send_rows.shape[1:], jnp.int32),
             pltpu.VMEM(multipoles.shape, jnp.bfloat16),
             pltpu.VMEM(top_local.shape, jnp.float32),
             pltpu.VMEM((2 * leaves, LANES), jnp.float32),
             pltpu.VMEM((total_rows, LANES), jnp.float32),
+            pltpu.VMEM((peers, pitch, LANES), jnp.bfloat16),
             pltpu.SemaphoreType.DMA((3,)),
+            pltpu.SemaphoreType.DMA((peers // PEER_GROUP,)),
         ],
         compiler_params=pltpu.CompilerParams(vmem_limit_bytes=60 * 2**20),
         name="send_rows",

time: 54.6 us -> 54.4 us (level)
  no operation moved by 1% of the time
where the time goes in v4:
time: 54.4 us; the launch traced here: 54.1 us
  Pallas kernels  27.7 us (51%)
  starting transfers between devices  13.6 us (25%)
  waiting for transfers between devices  11.7 us (22%)
  local copies, waits for them, and re-layouts  1.04 us (2%)
    pallas_call x1, Pallas kernels, on_device(): pl.pallas_call(functools.partial(main_kernel, peers), out_shape=jax.Shape...  24.6 us
    all_to_all x1, starting transfers between devices, on_device(): lax.all_to_all(outgoing, 'morton', split_axis=0, concat_axis=0, tiled=True)  8.73 us
    ppermute x1, waiting for transfers between devices, on_device(): low = lax.ppermute(multipoles[leaves // 2:], 'coef', forward)  4.21 us
    ppermute x1, waiting for transfers between devices, on_device(): high = lax.ppermute(multipoles[:leaves // 2], 'coef', backward)  4.07 us
    ppermute x1, starting transfers between devices, on_device(): low = lax.ppermute(multipoles[leaves // 2:], 'coef', forward)  3.55 us
    all_to_all x1, waiting for transfers between devices, on_device(): lax.all_to_all(outgoing, 'morton', split_axis=0, concat_axis=0, tiled=True)  3.39 us
    pallas_call x1, Pallas kernels, on_device(): pl.pallas_call(functools.partial(send_kernel, peers), out_shape=jax.Shape...  3.11 us
    ppermute x1, starting transfers between devices, on_device(): high = lax.ppermute(multipoles[:leaves // 2], 'coef', backward)  1.29 us
  transfers between devices with their start and end apart: 3, of which 3 were waited for; matrix products, arithmetic and copies ran while one was open for 2% of the time, Pallas kernels for 0%

profile of v4, /device:TPU:1, one launch (start us, length us, event | category | flops | bytes accessed | tf_op | source)
XLA Modules:
  0.0 54.1 jit_solution(7817382306357745611)
XLA Ops:
  0.0 3.1 %send_rows.1 = bf16[32,136,128]{2,1,0:T(8,128)(2,1)} custom-call(s32[1]{0:T(128)} %bitcast.3.me_ref, s32[1,32,64]{2,1,0:T(8,128)} %pick_hbm.1, bf16[1024,256]{1,0:T(8,128)(2,1)} %own_ref.1, f32[4,256]{1,0:T(4,128)} %top_hbm.1), custom_call_target="tpu_custom_call" | custom-call | tf_op jit(solution)/shard_map/send_rows/pallas_call | solution.py:240
  3.1 0.0 copy-start
  3.1 0.0 copy-start.2
  3.1 8.7 %all-to-all-start = ((bf16[32,136,128]{2,1,0:T(8,128)(2,1)}), bf16[32,136,128]{2,1,0:T(8,128)(2,1)S(1)}, u32[]{:S(2)}, u32[]{:S(2)}) async-start(bf16[32,136,128]{2,1,0:T(8,128)(2,1)} %send_rows.1), calls=%async_computation | async-start | bytes 2228224 | tf_op jit(solution)/shard_map/all_to_all | solution.py:258
  11.9 0.0 copy-done
  11.9 0.0 copy-start.3
  11.9 0.0 copy-start.1
  11.9 0.8 %fusion = (bf16[512,256]{1,0:T(8,128)(2,1)}, bf16[512,256]{1,0:T(8,128)(2,1)}) fusion(bf16[1024,256]{1,0:T(8,128)(2,1)S(1)} %copy-done), kind=kLoop, calls=%fused_computation.2 | loop fusion | bytes 1048576 | tf_op jit(solution)/shard_map/slice | solution.py:263
  12.8 3.5 %collective-permute-start = (bf16[512,256]{1,0:T(8,128)(2,1)}, bf16[512,256]{1,0:T(8,128)(2,1)S(1)}, u32[]{:S(2)}, u32[]{:S(2)}) collective-permute-start(bf16[512,256]{1,0:T(8,128)(2,1)} %get-tuple-element.6), channel_id=1, source_target_pairs={{0,1},{1,2},{2,3},{3,4},{4,5},{5,6},{6,7},{8,9},{9,10},{10,11},{11... | collective-permute-start | bytes 786440 | tf_op jit(solution)/shard_map/ppermute | solution.py:262
  16.3 1.3 %collective-permute-start.1 = (bf16[512,256]{1,0:T(8,128)(2,1)}, bf16[512,256]{1,0:T(8,128)(2,1)S(1)}, u32[]{:S(2)}, u32[]{:S(2)}) collective-permute-start(bf16[512,256]{1,0:T(8,128)(2,1)} %get-tuple-element.5), channel_id=1, source_target_pairs={{1,0},{2,1},{3,2},{4,3},{5,4},{6,5},{7,6},{9,8},{10,9},{11,10},{12... | collective-permute-start | bytes 786440 | tf_op jit(solution)/shard_map/ppermute | solution.py:263
  17.6 0.0 copy-done.2
  17.7 0.0 copy-done.3
  17.7 0.1 reshape.11
  17.9 4.2 %collective-permute-done.low_ref = bf16[512,256]{1,0:T(8,128)(2,1)S(1)} collective-permute-done((bf16[512,256]{1,0:T(8,128)(2,1)}, bf16[512,256]{1,0:T(8,128)(2,1)S(1)}, u32[]{:S(2)}, u32[]{:S(2)}) %collective-permute-start) | collective-permute-done | bytes 262176 | tf_op jit(solution)/shard_map/ppermute | solution.py:262
  22.1 4.1 %collective-permute-done.1.high_ref = bf16[512,256]{1,0:T(8,128)(2,1)S(1)} collective-permute-done((bf16[512,256]{1,0:T(8,128)(2,1)}, bf16[512,256]{1,0:T(8,128)(2,1)S(1)}, u32[]{:S(2)}, u32[]{:S(2)}) %collective-permute-start.1) | collective-permute-done | bytes 262176 | tf_op jit(solution)/shard_map/ppermute | solution.py:263
  26.1 3.4 %all-to-all-done.incoming_ref = bf16[32,136,128]{2,1,0:T(8,128)(2,1)S(1)} async-done(((bf16[32,136,128]{2,1,0:T(8,128)(2,1)}), bf16[32,136,128]{2,1,0:T(8,128)(2,1)S(1)}, u32[]{:S(2)}, u32[]{:S(2)}) %all-to-all-start) | async-done | bytes 1114144 | tf_op jit(solution)/shard_map/all_to_all | solution.py:258
  29.5 0.0 copy-done.1
  29.5 24.6 %far_field.1 = f32[1024,256]{1,0:T(8,128)} custom-call(s32[32768]{0:T(1024)S(1)} %bitcast.10, s32[8,128]{1,0:T(8,128)S(1)} %bitcast.11, bf16[512,256]{1,0:T(8,128)(2,1)S(1)} %collective-permute-done.low_ref, bf16[1024,256]{1,0:T(8,128)(2,1)S(1)} %copy-done, bf16[512,256]{1,0:T(8,128)(2,1)S(1)} %collective-permute-done.1.high_ref, ...), custom_call_target="tpu_custom_call" | custom-call | tf_op jit(solution)/shard_map/far_field/pallas_call | solution.py:269
  (4 shorter events, 0.1 us)
Async XLA Ops:
  3.1 8.8 %copy-start = (bf16[1024,256]{1,0:T(8,128)(2,1)S(1)}, bf16[1024,256]{1,0:T(8,128)(2,1)}, u32[]{:S(2)}) copy-start(bf16[1024,256]{1,0:T(8,128)(2,1)} %own_ref.1) | copy-start | bytes 1572868
  3.1 14.5 %copy-start.2 = (s32[1024,32]{0,1:T(8,128)S(1)}, s32[1024,32]{0,1:T(8,128)}, u32[]{:S(2)}) copy-start(s32[1024,32]{0,1:T(8,128)} %param.10) | copy-start | bytes 393220
  3.1 26.4 %all-to-all-start = ((bf16[32,136,128]{2,1,0:T(8,128)(2,1)}), bf16[32,136,128]{2,1,0:T(8,128)(2,1)S(1)}, u32[]{:S(2)}, u32[]{:S(2)}) async-start(bf16[32,136,128]{2,1,0:T(8,128)(2,1)} %send_rows.1), calls=%async_computation | async-start | bytes 2228224 | tf_op jit(solution)/shard_map/all_to_all | solution.py:258
  11.9 5.8 %copy-start.3 = (s32[1024]{0:T(1024)S(1)}, s32[1024]{0:T(1024)}, u32[]{:S(2)}) copy-start(s32[1024]{0:T(1024)} %param.13) | copy-start | bytes 12292
  11.9 17.6 %copy-start.1 = (bf16[8,256,256]{2,1,0:T(8,128)(2,1)S(1)}, bf16[8,256,256]{2,1,0:T(8,128)(2,1)}, u32[]{:S(2)}) copy-start(bf16[8,256,256]{2,1,0:T(8,128)(2,1)} %down_hbm.1) | copy-start | bytes 3145732
  12.8 9.3 %collective-permute-start = (bf16[512,256]{1,0:T(8,128)(2,1)}, bf16[512,256]{1,0:T(8,128)(2,1)S(1)}, u32[]{:S(2)}, u32[]{:S(2)}) collective-permute-start(bf16[512,256]{1,0:T(8,128)(2,1)} %get-tuple-element.6), channel_id=1, source_target_pairs={{0,1},{1,2},{2,3},{3,4},{4,5},{5,6},{6,7},{8,9},{9,10},{10,11},{11... | collective-permute-start | bytes 786440 | tf_op jit(solution)/shard_map/ppermute | solution.py:262
  16.3 9.8 %collective-permute-start.1 = (bf16[512,256]{1,0:T(8,128)(2,1)}, bf16[512,256]{1,0:T(8,128)(2,1)S(1)}, u32[]{:S(2)}, u32[]{:S(2)}) collective-permute-start(bf16[512,256]{1,0:T(8,128)(2,1)} %get-tuple-element.5), channel_id=1, source_target_pairs={{1,0},{2,1},{3,2},{4,3},{5,4},{6,5},{7,6},{9,8},{10,9},{11,10},{12... | collective-permute-start | bytes 786440 | tf_op jit(solution)/shard_map/ppermute | solution.py:263

commit v5 on v4

--- a/solution.py
+++ b/solution.py
@@ -13,7 +13,7 @@
 LANES = 128
 TARGETS = 512
 CLASSES = 32
-SLOT_ROWS = 1024
+SLOT_ROWS = 2048
 WINDOW = 4096
 BLANK = 2 * WINDOW
 
@@ -31,9 +31,13 @@
     copies = [
         pltpu.make_async_copy(source, target, sems.at[i])
         for i, (source, target) in enumerate(
-            ((pick_hbm.at[0], picks), (cells_hbm, cells), (top_hbm, top))
+            ((pick_hbm.at[0], picks), (top_hbm, top))
         )
     ]
+    quarter = cells.shape[0] // 4
+    for i in range(4):
+        part = pl.ds(i * quarter, quarter)
+        copies.append(pltpu.make_async_copy(cells_hbm.at[part], cells.at[part], sems.at[2 + i]))
     for copy in copies:
         copy.start()
     tops = 2 * top.shape[0]
@@ -42,10 +46,12 @@
     pitch = slab + tops
     for first in range(0, rows.shape[0], pitch):
         rows[first : first + pitch, :] = jnp.zeros((pitch, LANES), jnp.float32)
+    for i in range(4):
+        copies[2 + i].wait()
+        part = cells.at[pl.ds(i * quarter, quarter)]
+        split_rows(part, quarter, table, 2 * i * quarter)
     copies[0].wait()
     copies[1].wait()
-    split_rows(cells, cells.shape[0], table, 0)
-    copies[2].wait()
     for half in range(2):
         part = top[:, half * LANES : (half + 1) * LANES]
         for peer in range(peers):
@@ -249,7 +255,7 @@
             pltpu.VMEM((2 * leaves, LANES), jnp.float32),
             pltpu.VMEM((total_rows, LANES), jnp.float32),
             pltpu.VMEM((peers, pitch, LANES), jnp.bfloat16),
-            pltpu.SemaphoreType.DMA((3,)),
+            pltpu.SemaphoreType.DMA((6,)),
             pltpu.SemaphoreType.DMA((peers // PEER_GROUP,)),
         ],
         compiler_params=pltpu.CompilerParams(vmem_limit_bytes=60 * 2**20),

time: 54.4 us -> 53.8 us (0.989)
  Pallas kernels: 27.7 us -> 27.1 us
    pallas_call x1, Pallas kernels: 24.6 us -> 23.9 us  [on_device(): pl.pallas_call(functools.partial(main_kernel, peers), out_shape=jax.Shape...]
where the time goes in v5:
time: 53.8 us; the launch traced here: 53.5 us
  Pallas kernels  27.1 us (50%)
  starting transfers between devices  13.6 us (25%)
  waiting for transfers between devices  11.7 us (22%)
  local copies, waits for them, and re-layouts  1.04 us (2%)
    pallas_call x1, Pallas kernels, on_device(): pl.pallas_call(functools.partial(main_kernel, peers), out_shape=jax.Shape...  23.9 us
    all_to_all x1, starting transfers between devices, on_device(): lax.all_to_all(outgoing, 'morton', split_axis=0, concat_axis=0, tiled=True)  8.73 us
    ppermute x1, waiting for transfers between devices, on_device(): low = lax.ppermute(multipoles[leaves // 2:], 'coef', forward)  4.21 us
    ppermute x1, waiting for transfers between devices, on_device(): high = lax.ppermute(multipoles[:leaves // 2], 'coef', backward)  4.07 us
    ppermute x1, starting transfers between devices, on_device(): low = lax.ppermute(multipoles[leaves // 2:], 'coef', forward)  3.55 us
    all_to_all x1, waiting for transfers between devices, on_device(): lax.all_to_all(outgoing, 'morton', split_axis=0, concat_axis=0, tiled=True)  3.39 us
    pallas_call x1, Pallas kernels, on_device(): pl.pallas_call(functools.partial(send_kernel, peers), out_shape=jax.Shape...  3.17 us
    ppermute x1, starting transfers between devices, on_device(): high = lax.ppermute(multipoles[:leaves // 2], 'coef', backward)  1.29 us
  transfers between devices with their start and end apart: 3, of which 3 were waited for; matrix products, arithmetic and copies ran while one was open for 2% of the time, Pallas kernels for 0%

profile of v5, /device:TPU:1, one launch (start us, length us, event | category | flops | bytes accessed | tf_op | source)
XLA Modules:
  0.0 53.5 jit_solution(8540078516133129509)
XLA Ops:
  0.0 3.2 %send_rows.1 = bf16[32,136,128]{2,1,0:T(8,128)(2,1)} custom-call(s32[1]{0:T(128)} %bitcast.3.me_ref, s32[1,32,64]{2,1,0:T(8,128)} %pick_hbm.1, bf16[1024,256]{1,0:T(8,128)(2,1)} %own_ref.1, f32[4,256]{1,0:T(4,128)} %top_hbm.1), custom_call_target="tpu_custom_call" | custom-call | tf_op jit(solution)/shard_map/send_rows/pallas_call | solution.py:246
  3.2 0.0 copy-start
  3.2 0.0 copy-start.2
  3.2 8.7 %all-to-all-start = ((bf16[32,136,128]{2,1,0:T(8,128)(2,1)}), bf16[32,136,128]{2,1,0:T(8,128)(2,1)S(1)}, u32[]{:S(2)}, u32[]{:S(2)}) async-start(bf16[32,136,128]{2,1,0:T(8,128)(2,1)} %send_rows.1), calls=%async_computation | async-start | bytes 2228224 | tf_op jit(solution)/shard_map/all_to_all | solution.py:264
  11.9 0.0 copy-done
  11.9 0.0 copy-start.3
  12.0 0.0 copy-start.1
  12.0 0.8 %fusion = (bf16[512,256]{1,0:T(8,128)(2,1)}, bf16[512,256]{1,0:T(8,128)(2,1)}) fusion(bf16[1024,256]{1,0:T(8,128)(2,1)S(1)} %copy-done), kind=kLoop, calls=%fused_computation.2 | loop fusion | bytes 1048576 | tf_op jit(solution)/shard_map/slice | solution.py:269
  12.8 3.5 %collective-permute-start = (bf16[512,256]{1,0:T(8,128)(2,1)}, bf16[512,256]{1,0:T(8,128)(2,1)S(1)}, u32[]{:S(2)}, u32[]{:S(2)}) collective-permute-start(bf16[512,256]{1,0:T(8,128)(2,1)} %get-tuple-element.6), channel_id=1, source_target_pairs={{0,1},{1,2},{2,3},{3,4},{4,5},{5,6},{6,7},{8,9},{9,10},{10,11},{11... | collective-permute-start | bytes 786440 | tf_op jit(solution)/shard_map/ppermute | solution.py:268
  16.4 1.3 %collective-permute-start.1 = (bf16[512,256]{1,0:T(8,128)(2,1)}, bf16[512,256]{1,0:T(8,128)(2,1)S(1)}, u32[]{:S(2)}, u32[]{:S(2)}) collective-permute-start(bf16[512,256]{1,0:T(8,128)(2,1)} %get-tuple-element.5), channel_id=1, source_target_pairs={{1,0},{2,1},{3,2},{4,3},{5,4},{6,5},{7,6},{9,8},{10,9},{11,10},{12... | collective-permute-start | bytes 786440 | tf_op jit(solution)/shard_map/ppermute | solution.py:269
  17.7 0.0 copy-done.2
  17.8 0.0 copy-done.3
  17.8 0.1 reshape.11
  17.9 4.2 %collective-permute-done.low_ref = bf16[512,256]{1,0:T(8,128)(2,1)S(1)} collective-permute-done((bf16[512,256]{1,0:T(8,128)(2,1)}, bf16[512,256]{1,0:T(8,128)(2,1)S(1)}, u32[]{:S(2)}, u32[]{:S(2)}) %collective-permute-start) | collective-permute-done | bytes 262176 | tf_op jit(solution)/shard_map/ppermute | solution.py:268
  22.1 4.1 %collective-permute-done.1.high_ref = bf16[512,256]{1,0:T(8,128)(2,1)S(1)} collective-permute-done((bf16[512,256]{1,0:T(8,128)(2,1)}, bf16[512,256]{1,0:T(8,128)(2,1)S(1)}, u32[]{:S(2)}, u32[]{:S(2)}) %collective-permute-start.1) | collective-permute-done | bytes 262176 | tf_op jit(solution)/shard_map/ppermute | solution.py:269
  26.2 3.4 %all-to-all-done.incoming_ref = bf16[32,136,128]{2,1,0:T(8,128)(2,1)S(1)} async-done(((bf16[32,136,128]{2,1,0:T(8,128)(2,1)}), bf16[32,136,128]{2,1,0:T(8,128)(2,1)S(1)}, u32[]{:S(2)}, u32[]{:S(2)}) %all-to-all-start) | async-done | bytes 1114144 | tf_op jit(solution)/shard_map/all_to_all | solution.py:264
  29.6 0.0 copy-done.1
  29.6 23.9 %far_field.1 = f32[1024,256]{1,0:T(8,128)} custom-call(s32[32768]{0:T(1024)S(1)} %bitcast.10, s32[8,128]{1,0:T(8,128)S(1)} %bitcast.11, bf16[512,256]{1,0:T(8,128)(2,1)S(1)} %collective-permute-done.low_ref, bf16[1024,256]{1,0:T(8,128)(2,1)S(1)} %copy-done, bf16[512,256]{1,0:T(8,128)(2,1)S(1)} %collective-permute-done.1.high_ref, ...), custom_call_target="tpu_custom_call" | custom-call | tf_op jit(solution)/shard_map/far_field/pallas_call | solution.py:275
  (4 shorter events, 0.1 us)
Async XLA Ops:
  3.2 8.8 %copy-start = (bf16[1024,256]{1,0:T(8,128)(2,1)S(1)}, bf16[1024,256]{1,0:T(8,128)(2,1)}, u32[]{:S(2)}) copy-start(bf16[1024,256]{1,0:T(8,128)(2,1)} %own_ref.1) | copy-start | bytes 1572868
  3.2 14.5 %copy-start.2 = (s32[1024,32]{0,1:T(8,128)S(1)}, s32[1024,32]{0,1:T(8,128)}, u32[]{:S(2)}) copy-start(s32[1024,32]{0,1:T(8,128)} %param.10) | copy-start | bytes 393220
  3.2 26.4 %all-to-all-start = ((bf16[32,136,128]{2,1,0:T(8,128)(2,1)}), bf16[32,136,128]{2,1,0:T(8,128)(2,1)S(1)}, u32[]{:S(2)}, u32[]{:S(2)}) async-start(bf16[32,136,128]{2,1,0:T(8,128)(2,1)} %send_rows.1), calls=%async_computation | async-start | bytes 2228224 | tf_op jit(solution)/shard_map/all_to_all | solution.py:264
  11.9 5.8 %copy-start.3 = (s32[1024]{0:T(1024)S(1)}, s32[1024]{0:T(1024)}, u32[]{:S(2)}) copy-start(s32[1024]{0:T(1024)} %param.13) | copy-start | bytes 12292
  12.0 17.6 %copy-start.1 = (bf16[8,256,256]{2,1,0:T(8,128)(2,1)S(1)}, bf16[8,256,256]{2,1,0:T(8,128)(2,1)}, u32[]{:S(2)}) copy-start(bf16[8,256,256]{2,1,0:T(8,128)(2,1)} %down_hbm.1) | copy-start | bytes 3145732
  12.8 9.3 %collective-permute-start = (bf16[512,256]{1,0:T(8,128)(2,1)}, bf16[512,256]{1,0:T(8,128)(2,1)S(1)}, u32[]{:S(2)}, u32[]{:S(2)}) collective-permute-start(bf16[512,256]{1,0:T(8,128)(2,1)} %get-tuple-element.6), channel_id=1, source_target_pairs={{0,1},{1,2},{2,3},{3,4},{4,5},{5,6},{6,7},{8,9},{9,10},{10,11},{11... | collective-permute-start | bytes 786440 | tf_op jit(solution)/shard_map/ppermute | solution.py:268
  16.4 9.8 %collective-permute-start.1 = (bf16[512,256]{1,0:T(8,128)(2,1)}, bf16[512,256]{1,0:T(8,128)(2,1)S(1)}, u32[]{:S(2)}, u32[]{:S(2)}) collective-permute-start(bf16[512,256]{1,0:T(8,128)(2,1)} %get-tuple-element.5), channel_id=1, source_target_pairs={{1,0},{2,1},{3,2},{4,3},{5,4},{6,5},{7,6},{9,8},{10,9},{11,10},{12... | collective-permute-start | bytes 786440 | tf_op jit(solution)/shard_map/ppermute | solution.py:269
